TPU v7x, 128 devices: a whole 4x4x4 slice. The times are simulated.
128 devices in a mesh: dp: 2 (over core), expert: 64 (over z, x, y).
Axes of the slice: x: 4, y: 4, z: 4, core: 2. Of those that a mesh axis runs over, the one named last changes fastest.
Arguments:
- tokens: bfloat16 [16384, 2048], P(('dp', 'expert')), may hold values from -6 to 6
- route_ids: int32 [16384, 8], P(('dp', 'expert')), may hold values from 0 to 63, all different within a row; in each aligned block of 128 rows (0 to 127, 128 to 255, ...) at most 28 rows name the same one
- route_probs: float32 [16384, 8], P(('dp', 'expert')), may hold values from 0.02 to 0.4
- cotangent: bfloat16 [16384, 2048], P(('dp', 'expert')), may hold values from -6 to 6
- w_gate: bfloat16 [64, 2048, 768], P('expert'), may hold values from -0.125 to 0.125
- w_up: bfloat16 [64, 2048, 768], P('expert'), may hold values from -0.125 to 0.125
- w_down: bfloat16 [64, 768, 2048], P('expert'), may hold values from -0.21875 to 0.21875
Outputs:
- mixed: bfloat16 [16384, 2048], P(('dp', 'expert'))
- grad_tokens: bfloat16 [16384, 2048], P(('dp', 'expert'))
- grad_probs: float32 [16384, 8], P(('dp', 'expert'))
- grad_gate: bfloat16 [64, 2048, 768], P('expert', None, 'dp')
- grad_up: bfloat16 [64, 2048, 768], P('expert', None, 'dp')
- grad_down: bfloat16 [64, 768, 2048], P('expert', None, 'dp')
Inputs may be any that keep to these rules, and one draw needn't show every extreme that they name: `route_ids`: each token names 8 different experts. Among the 128 tokens of one device (aligned blocks of rows), no expert is named more than 28 times, a bound that some block reaches.
All inputs are finite; a program needn't handle non-finite values.
Results may differ from a plain program's by a relative error of at most 0.012.
Values may be sent and summed in bfloat16 or wider, within the bound.
A program may use at most 256 MiB of HBM per device.

v0:
```python
import jax
import jax.numpy as jnp
from jax import lax
from jax.sharding import PartitionSpec as P

BLOCK = 128


def silu_parts(gate_pre):
    sigmoid = jax.nn.sigmoid(gate_pre)
    return (gate_pre * sigmoid, sigmoid * (1.0 + gate_pre * (1.0 - sigmoid)))


def contract_last(left_side, right_side):
    return lax.dot_general(
        left_side, right_side, (((1,), (1,)), ((), ())), preferred_element_type=jnp.float32
    )


def contract_rows(left_side, right_side):
    return lax.dot_general(
        left_side, right_side, (((0,), (0,)), ((), ())), preferred_element_type=jnp.float32
    )


def pack_tables(counts, slot_width, capacity):
    source_count = counts.shape[0]
    run_ends = jnp.cumsum(counts)
    run_starts = run_ends - counts
    row_ids = jnp.arange(capacity, dtype=jnp.int32)
    source_of = jnp.minimum(
        jnp.sum((run_ends[None, :] <= row_ids[:, None]).astype(jnp.int32), axis=1), source_count - 1
    )
    total_rows = run_ends[source_count - 1]
    is_live = row_ids < total_rows
    gather_at = jnp.where(is_live, source_of * slot_width + row_ids - run_starts[source_of], 0)
    slot_ids = jnp.arange(slot_width, dtype=jnp.int32)
    unpack_at = (run_starts[:, None] + slot_ids[None, :]).reshape(-1)
    unpack_live = (slot_ids[None, :] < counts[:, None]).reshape(-1)
    return (gather_at, is_live, unpack_at, unpack_live, total_rows)


def to_sources(returned):
    return lax.all_to_all(returned, "expert", split_axis=0, concat_axis=0, tiled=True)


def body(tokens, route_ids, route_probs, cotangent, w_gate, w_up, w_down):
    tok_rows, features = tokens.shape
    top_k = route_ids.shape[1]
    expert_count = lax.axis_size("expert")
    capacity_slots = 7 * tok_rows * top_k // (4 * expert_count)
    pair_count = tok_rows * top_k
    flat_ids = route_ids.reshape(pair_count)
    hit_table = (flat_ids[:, None] == jnp.arange(expert_count, dtype=jnp.int32)[None, :]).astype(
        jnp.int32
    )
    position = jnp.sum((jnp.cumsum(hit_table, axis=0) - 1) * hit_table, axis=1)
    counts = jnp.sum(hit_table, axis=0)
    slot_index = flat_ids * capacity_slots + position
    total_slots = expert_count * capacity_slots

    def to_slots(values):
        placed = jnp.zeros((total_slots, features), jnp.bfloat16).at[slot_index].set(values)
        return placed.reshape(expert_count, capacity_slots, features)

    send_inputs = to_slots(jnp.repeat(tokens, top_k, axis=0))
    count_high = (counts // 128).astype(jnp.float32).astype(jnp.bfloat16)
    count_low = (counts % 128).astype(jnp.float32).astype(jnp.bfloat16)
    recv_inputs, recv_high, recv_low = (
        lax.all_to_all(send_inputs, "expert", split_axis=0, concat_axis=0, tiled=True),
        lax.all_to_all(count_high, "expert", split_axis=0, concat_axis=0, tiled=True),
        lax.all_to_all(count_low, "expert", split_axis=0, concat_axis=0, tiled=True),
    )
    recv_counts = recv_high.astype(jnp.int32) * 128 + recv_low.astype(jnp.int32)
    capacity = (total_slots + BLOCK - 1) // BLOCK * BLOCK
    gather_at, is_live, unpack_at, unpack_live, total_rows = pack_tables(
        recv_counts, capacity_slots, capacity
    )
    packed_inputs = jnp.where(
        is_live[:, None],
        recv_inputs.reshape(total_slots, features)[gather_at],
        jnp.zeros((), jnp.bfloat16),
    )
    block_total = (total_rows + BLOCK - 1) // BLOCK
    gate_matrix = w_gate[0]
    up_matrix = w_up[0]
    down_matrix = w_down[0]
    hidden_width = gate_matrix.shape[1]

    def forward_block(block_index, carried):
        out_rows, gate_rows, up_rows = carried
        row_start = block_index * BLOCK
        row_inputs = lax.dynamic_slice_in_dim(packed_inputs, row_start, BLOCK, 0)
        gate_pre = jnp.dot(row_inputs, gate_matrix, preferred_element_type=jnp.float32)
        up_pre = jnp.dot(row_inputs, up_matrix, preferred_element_type=jnp.float32)
        activation, derivative = silu_parts(gate_pre)
        hidden = (activation * up_pre).astype(jnp.bfloat16)
        outputs = jnp.dot(hidden, down_matrix, preferred_element_type=jnp.float32).astype(
            jnp.bfloat16
        )
        out_rows = lax.dynamic_update_slice_in_dim(out_rows, outputs, row_start, 0)
        gate_rows = lax.dynamic_update_slice_in_dim(gate_rows, gate_pre, row_start, 0)
        up_rows = lax.dynamic_update_slice_in_dim(up_rows, up_pre, row_start, 0)
        return (out_rows, gate_rows, up_rows)

    forward_start = (
        jnp.zeros((capacity, features), jnp.bfloat16),
        jnp.zeros((capacity, hidden_width), jnp.float32),
        jnp.zeros((capacity, hidden_width), jnp.float32),
    )
    out_rows, gate_rows, up_rows = lax.fori_loop(0, block_total, forward_block, forward_start)

    def unpack(rows_packed):
        spread = jnp.where(
            unpack_live[:, None], rows_packed[unpack_at], jnp.zeros((), jnp.bfloat16)
        )
        return spread.reshape(expert_count, capacity_slots, features)

    returned_out = to_sources(unpack(out_rows)).reshape(total_slots, features)
    expert_out = returned_out[slot_index].reshape(tok_rows, top_k, features)
    mixed = jnp.einsum(
        "tk,tkd->td", route_probs, expert_out, preferred_element_type=jnp.float32
    ).astype(jnp.bfloat16)
    grad_probs = jnp.einsum("tkd,td->tk", expert_out, cotangent, preferred_element_type=jnp.float32)
    grad_out = (
        (route_probs[:, :, None] * cotangent[:, None, :])
        .astype(jnp.bfloat16)
        .reshape(pair_count, features)
    )
    send_grads = to_slots(grad_out)
    recv_grads = lax.all_to_all(send_grads, "expert", split_axis=0, concat_axis=0, tiled=True)
    packed_grads = jnp.where(
        is_live[:, None],
        recv_grads.reshape(total_slots, features)[gather_at],
        jnp.zeros((), jnp.bfloat16),
    )

    def block_pieces(row_start):
        row_grads = lax.dynamic_slice_in_dim(packed_grads, row_start, BLOCK, 0)
        gate_pre = lax.dynamic_slice_in_dim(gate_rows, row_start, BLOCK, 0)
        up_pre = lax.dynamic_slice_in_dim(up_rows, row_start, BLOCK, 0)
        activation, derivative = silu_parts(gate_pre)
        hidden = (activation * up_pre).astype(jnp.bfloat16)
        grad_hidden = contract_last(row_grads, down_matrix)
        grad_gate_pre = (grad_hidden * up_pre * derivative).astype(jnp.bfloat16)
        grad_up_pre = (grad_hidden * activation).astype(jnp.bfloat16)
        grad_rows = (
            contract_last(grad_gate_pre, gate_matrix) + contract_last(grad_up_pre, up_matrix)
        ).astype(jnp.bfloat16)
        return (row_grads, hidden, grad_gate_pre, grad_up_pre, grad_rows)

    def store_block(block_index, carried):
        grad_rows_all, hidden_all, gate_grad_all, up_grad_all = carried
        row_start = block_index * BLOCK
        row_grads, hidden, grad_gate_pre, grad_up_pre, grad_rows = block_pieces(row_start)
        grad_rows_all = lax.dynamic_update_slice_in_dim(grad_rows_all, grad_rows, row_start, 0)
        hidden_all = lax.dynamic_update_slice_in_dim(hidden_all, hidden, row_start, 0)
        gate_grad_all = lax.dynamic_update_slice_in_dim(gate_grad_all, grad_gate_pre, row_start, 0)
        up_grad_all = lax.dynamic_update_slice_in_dim(up_grad_all, grad_up_pre, row_start, 0)
        return (grad_rows_all, hidden_all, gate_grad_all, up_grad_all)

    store_start = (
        jnp.zeros((capacity, features), jnp.bfloat16),
        jnp.zeros((capacity, hidden_width), jnp.bfloat16),
        jnp.zeros((capacity, hidden_width), jnp.bfloat16),
        jnp.zeros((capacity, hidden_width), jnp.bfloat16),
    )
    grad_rows_all, hidden_all, gate_grad_all, up_grad_all = lax.fori_loop(
        0, block_total, store_block, store_start
    )
    acc_gate = contract_rows(packed_inputs, gate_grad_all)
    acc_up = contract_rows(packed_inputs, up_grad_all)
    acc_down = contract_rows(hidden_all, packed_grads)
    grad_gate, grad_up, grad_down = (
        lax.psum_scatter(
            acc_gate[None].astype(jnp.bfloat16), "dp", scatter_dimension=2, tiled=True
        ).astype(jnp.float32),
        lax.psum_scatter(
            acc_up[None].astype(jnp.bfloat16), "dp", scatter_dimension=2, tiled=True
        ).astype(jnp.float32),
        lax.psum_scatter(
            acc_down[None].astype(jnp.bfloat16), "dp", scatter_dimension=2, tiled=True
        ).astype(jnp.float32),
    )
    returned_grads = to_sources(unpack(grad_rows_all)).reshape(total_slots, features)
    grad_pairs = returned_grads[slot_index].reshape(tok_rows, top_k, features)
    grad_tokens = jnp.sum(grad_pairs.astype(jnp.float32), axis=1).astype(jnp.bfloat16)
    return (
        mixed,
        grad_tokens,
        grad_probs,
        grad_gate.astype(jnp.bfloat16),
        grad_up.astype(jnp.bfloat16),
        grad_down.astype(jnp.bfloat16),
    )


def solution(mesh):
    return jax.shard_map(
        body,
        mesh=mesh,
        in_specs=(
            P(("dp", "expert"), None),
            P(("dp", "expert"), None),
            P(("dp", "expert"), None),
            P(("dp", "expert"), None),
            P("expert", None, None),
            P("expert", None, None),
            P("expert", None, None),
        ),
        out_specs=(
            P(("dp", "expert"), None),
            P(("dp", "expert"), None),
            P(("dp", "expert"), None),
            P("expert", None, "dp"),
            P("expert", None, "dp"),
            P("expert", None, "dp"),
        ),
        check_vma=False,
    )
```

profile of v0, /device:TPU:2, one launch (start us, length us, event | category | flops | bytes accessed | tf_op | source)
XLA Modules:
  0.0 952.8 jit_solution(1641643288089728090)
XLA Ops:
  8.2 18.0 %reduce-window.11 = s32[64,8,128]{2,1,0:T(8,128)S(1)} reduce-window(s32[64,8,128]{2,1,0:T(8,128)S(1)} %fusion.36, s32[]{:T(128)} %constant.79.clone.1), window={size=1x1x128 pad=0_0x0_0x127_0}, to_apply=%region_2.3 | reduce-window | flops 8323072 | bytes 524292 | tf_op jit(solution)/shard_map/reduce-window.1
  27.7 11.5 %all-to-all-start = ((bf16[64,1,1]{2,1,0:T(2,128)(2,1)}), bf16[64,1,1]{2,1,0:T(2,128)(2,1)S(1)}, u32[]{:S(2)}, u32[]{:S(2)}) async-start(bf16[64,1,1]{2,1,0:T(2,128)(2,1)} %copy.33), calls=%async_computation | async-start | bytes 65536 | tf_op jit(solution)/shard_map/all_to_all | solution.py:71
  40.9 6.8 all-to-all-done
  47.7 5.9 all-to-all-start.1
  53.7 10.8 %scatter_custom_fusion = bf16[1792,2048]{1,0:T(8,128)(2,1)} fusion(s32[1024]{0:T(1024)S(1)} %bitcast.188, bf16[]{:T(256)} %constant.85.clone.1, bf16[128,2048]{1,0:T(8,128)(2,1)S(1)} %copy-done), kind=kCustom, calls=%fused_computation.47 | custom fusion | bytes 7864322 | tf_op jit(solution)/shard_map/scatter | solution.py:63
  64.4 10.8 %reshape.356 = bf16[64,28,2048]{2,1,0:T(8,128)(2,1)} reshape(bf16[1792,2048]{1,0:T(8,128)(2,1)} %scatter_custom_fusion) | data formatting | bytes 14680064 | tf_op jit(solution)/shard_map/reshape | solution.py:64
  75.2 11.0 %all-to-all-start.2 = ((bf16[64,28,2048]{2,1,0:T(8,128)(2,1)}), bf16[64,28,2048]{2,1,0:T(8,128)(2,1)}, u32[]{:S(2)}, u32[]{:S(2)}) async-start(bf16[64,28,2048]{2,1,0:T(8,128)(2,1)} %reshape.356), calls=%async_computation.2 | async-start | bytes 16777216 | tf_op jit(solution)/shard_map/all_to_all | solution.py:70
  86.6 11.2 %scatter_custom_fusion.1 = bf16[1792,2048]{1,0:T(8,128)(2,1)} fusion(s32[1024]{0:T(1024)S(1)} %bitcast.189, f32[128,2048]{1,0:T(8,128)S(1)} %convert_element_type.149, f32[1024]{0:T(1024)S(1)} %mul.108, bf16[]{:T(256)} %constant.85.clone.1), kind=kCustom, calls=%fused_computation.41 | custom fusion | flops 4194304 | bytes 8392706 | tf_op jit(solution)/shard_map/scatter | solution.py:63
  97.8 10.8 %reshape.360 = bf16[64,28,2048]{2,1,0:T(8,128)(2,1)} reshape(bf16[1792,2048]{1,0:T(8,128)(2,1)} %scatter_custom_fusion.1) | data formatting | bytes 14680064 | tf_op jit(solution)/shard_map/reshape | solution.py:64
  108.6 90.2 %all-to-all-done.2 = bf16[64,28,2048]{2,1,0:T(8,128)(2,1)} async-done(((bf16[64,28,2048]{2,1,0:T(8,128)(2,1)}), bf16[64,28,2048]{2,1,0:T(8,128)(2,1)}, u32[]{:S(2)}, u32[]{:S(2)}) %all-to-all-start.2) | async-done | bytes 7340064 | tf_op jit(solution)/shard_map/all_to_all | solution.py:70
  198.8 9.9 %all-to-all-start.4 = ((bf16[64,28,2048]{2,1,0:T(8,128)(2,1)}), bf16[64,28,2048]{2,1,0:T(8,128)(2,1)}, u32[]{:S(2)}, u32[]{:S(2)}) async-start(bf16[64,28,2048]{2,1,0:T(8,128)(2,1)} %reshape.360), calls=%async_computation.4 | async-start | bytes 16777216 | tf_op jit(solution)/shard_map/all_to_all | solution.py:131
  212.3 4.4 fusion.37
  219.4 35.2 %select_select_fusion = s32[1792]{0:T(1024)S(1)} fusion(pred[1792]{0:T(1024)(128)(4,1)S(1)} %get-tuple-element.185, pred[1792]{0:T(1024)(128)(4,1)S(1)} %get-tuple-element.184, pred[1792]{0:T(1024)(128)(4,1)S(1)} %get-tuple-element.183, pred[1792]{0:T(1024)(128)(4,1)S(1)} %get-tuple-element.182, pred[1792]{0:T(1024)(128)(4,1)S(1)} %get-tuple-element.181, ...), kind=kLoop, calls=%fused_computation.148 | loop fusion | flops 102144 | bytes 116708 | tf_op jit(solution)/shard_map/gather | solution.py:36
  256.0 10.9 %reshape.357 = bf16[1792,2048]{1,0:T(8,128)(2,1)} reshape(bf16[64,28,2048]{2,1,0:T(8,128)(2,1)} %all-to-all-done.2) | data formatting | bytes 14680064 | tf_op jit(solution)/shard_map/reshape | solution.py:81
  266.9 18.6 %gather_fusion = bf16[1792,2048]{1,0:T(8,128)(2,1)} fusion(bf16[1792,2048]{1,0:T(8,128)(2,1)} %reshape.357, s32[2048]{0:T(1024)S(1)} %pad_clamp_fusion.1), kind=kCustom, calls=%fused_computation | custom fusion | bytes 14687232 | tf_op jit(solution)/shard_map/gather | solution.py:81
  285.5 27.7 %all-to-all-done.4 = bf16[64,28,2048]{2,1,0:T(8,128)(2,1)} async-done(((bf16[64,28,2048]{2,1,0:T(8,128)(2,1)}), bf16[64,28,2048]{2,1,0:T(8,128)(2,1)}, u32[]{:S(2)}, u32[]{:S(2)}) %all-to-all-start.4) | async-done | bytes 7340064 | tf_op jit(solution)/shard_map/all_to_all | solution.py:131
  313.2 11.0 %reshape.361 = bf16[1792,2048]{1,0:T(8,128)(2,1)} reshape(bf16[64,28,2048]{2,1,0:T(8,128)(2,1)} %all-to-all-done.4) | data formatting | bytes 14680064 | tf_op jit(solution)/shard_map/reshape | solution.py:134
  324.1 18.6 %gather_fusion.3 = bf16[1792,2048]{1,0:T(8,128)(2,1)} fusion(bf16[1792,2048]{1,0:T(8,128)(2,1)} %reshape.361, s32[2048]{0:T(1024)S(1)} %pad_clamp_fusion.1), kind=kCustom, calls=%fused_computation.3 | custom fusion | bytes 14687232 | tf_op jit(solution)/shard_map/gather | solution.py:134
  342.7 10.7 %broadcast_select_fusion.2 = (bf16[1792,2048]{1,0:T(8,128)(2,1)}, bf16[1792,2048]{1,0:T(8,128)(2,1)}) fusion(bf16[1792,2048]{1,0:T(8,128)(2,1)} %gather_fusion.3, pred[1792]{0:T(1024)(128)(4,1)S(1)} %iota_compare_fusion.4, bf16[1792,2048]{1,0:T(8,128)(2,1)} %gather_fusion), kind=kLoop, calls=%fused_computation.39 | loop fusion | flops 7340032 | bytes 29361920 | tf_op jit(solution)/shard_map/jit(_where)/select_n | solution.py:132
  353.4 3.9 broadcast.270.clone
  357.3 2.8 broadcast.271
  360.2 2.7 broadcast.271.clone
  362.9 44.0 %while.30 = (s32[]{:T(128)}, bf16[1792,2048]{1,0:T(8,128)(2,1)}, f32[1792,768]{1,0:T(8,128)}, f32[1792,768]{1,0:T(8,128)}, s32[]{:T(128)}, /*index=5*/bf16[1792,...) while((s32[]{:T(128)}, bf16[1792,2048]{1,0:T(8,128)(2,1)}, ...), condition=%wide.region_8.9_spmd, body=%wide.region_7.8_spmd.sunk | while | flops 1208811520 | bytes 38537444 | solution.py:111
  362.9 3.6 constant_dynamic-update-slice_fusion.7
  370.2 3.5 constant_dynamic-update-slice_fusion.7
  377.6 3.5 constant_dynamic-update-slice_fusion.7
  384.9 3.5 constant_dynamic-update-slice_fusion.7
  392.2 3.5 constant_dynamic-update-slice_fusion.7
  399.6 3.5 constant_dynamic-update-slice_fusion.7
  406.9 4.0 broadcast.270
  414.4 45.2 %while.31 = (s32[]{:T(128)}, bf16[1792,2048]{1,0:T(8,128)(2,1)}, bf16[1792,768]{1,0:T(8,128)(2,1)S(1)}, bf16[1792,768]{1,0:T(8,128)(2,1)}, bf16[1792,768]{1,0:T(...) while((s32[]{:T(128)}, bf16[1792,2048]{1,0:T(8,128)(2,1)}, ...), condition=%wide.region_11.12_spmd, body=%wide.region_10.11_spmd.sunk | while | flops 1209958400 | bytes 39912700 | solution.py:168
  414.5 4.3 constant_dynamic-update-slice_fusion.9
  421.9 4.3 constant_dynamic-update-slice_fusion.9
  429.3 4.3 constant_dynamic-update-slice_fusion.9
  436.8 4.3 constant_dynamic-update-slice_fusion.9
  444.4 4.3 constant_dynamic-update-slice_fusion.9
  451.8 4.3 constant_dynamic-update-slice_fusion.9
  459.7 10.3 %fusion.30 = bf16[1,2048,768]{2,1,0:T(8,128)(2,1)} fusion(bf16[1792,2048]{1,0:T(8,128)(2,1)} %get-tuple-element.563, bf16[1792,768]{1,0:T(8,128)(2,1)} %get-tuple-element.127), kind=kOutput, calls=%fused_computation.61 | convolution fusion | flops 5638717440 | bytes 13238272 | tf_op jit(solution)/shard_map/dot_general | solution.py:21
  470.0 15.8 %copy.49 = bf16[1,2048,768]{1,0,2:T(2,128)(2,1)} copy(bf16[1,2048,768]{2,1,0:T(8,128)(2,1)} %fusion.30) | data formatting | bytes 6291456
  485.7 6.4 copy.60
  492.4 18.6 %gather_fusion.4 = bf16[1792,2048]{1,0:T(8,128)(2,1)} fusion(bf16[1792,2048]{1,0:T(8,128)(2,1)} %get-tuple-element.125, s32[2048]{0:T(1024)S(1)} %pad_clamp_fusion), kind=kCustom, calls=%fused_computation.4 | custom fusion | bytes 14687232 | tf_op jit(solution)/shard_map/gather | solution.py:115
  511.1 10.2 %gather.35 = bf16[64,28,2048]{2,1,0:T(8,128)(2,1)} reshape(bf16[1792,2048]{1,0:T(8,128)(2,1)} %gather_fusion.4) | data formatting | bytes 14680064 | tf_op jit(solution)/shard_map/gather | solution.py:115
  521.3 18.6 %gather_fusion.1 = bf16[1792,2048]{1,0:T(8,128)(2,1)} fusion(bf16[1792,2048]{1,0:T(8,128)(2,1)} %get-tuple-element.122, s32[2048]{0:T(1024)S(1)} %pad_clamp_fusion), kind=kCustom, calls=%fused_computation.1 | custom fusion | bytes 14687232 | tf_op jit(solution)/shard_map/gather | solution.py:115
  539.8 10.8 %gather.31 = bf16[64,28,2048]{2,1,0:T(8,128)(2,1)} reshape(bf16[1792,2048]{1,0:T(8,128)(2,1)} %gather_fusion.1) | data formatting | bytes 14680064 | tf_op jit(solution)/shard_map/gather | solution.py:115
  550.7 11.6 %broadcast_select_fusion = (bf16[64,28,2048]{2,1,0:T(8,128)(2,1)}, bf16[64,28,2048]{2,1,0:T(8,128)(2,1)}) fusion(bf16[64,28,2048]{2,1,0:T(8,128)(2,1)} %gather.35, pred[64,28]{1,0:T(8,128)(4,1)S(1)} %iota_compare_fusion.3, bf16[64,28,2048]{2,1,0:T(8,128)(2,1)} %gather.31), kind=kLoop, calls=%fused_computation.37 | loop fusion | flops 7340032 | bytes 29361920 | tf_op jit(solution)/shard_map/jit(_where)/select_n | solution.py:114
  562.3 127.6 %all-to-all-start.5 = ((bf16[64,28,2048]{2,1,0:T(8,128)(2,1)}), bf16[64,28,2048]{2,1,0:T(8,128)(2,1)}, u32[]{:S(2)}, u32[]{:S(2)}) async-start(bf16[64,28,2048]{2,1,0:T(8,128)(2,1)} %get-tuple-element.243), calls=%async_computation.5 | async-start | bytes 16777216 | tf_op jit(solution)/shard_map/all_to_all | solution.py:44
  689.9 10.3 %fusion.29 = bf16[1,2048,768]{2,1,0:T(8,128)(2,1)} fusion(bf16[1792,2048]{1,0:T(8,128)(2,1)} %get-tuple-element.563, bf16[1792,768]{1,0:T(8,128)(2,1)} %get-tuple-element.126), kind=kOutput, calls=%fused_computation.60 | convolution fusion | flops 5638717440 | bytes 13238272 | tf_op jit(solution)/shard_map/dot_general | solution.py:21
  700.1 15.8 %copy.47 = bf16[1,2048,768]{1,0,2:T(2,128)(2,1)} copy(bf16[1,2048,768]{2,1,0:T(8,128)(2,1)} %fusion.29) | data formatting | bytes 6291456
  715.9 6.4 copy.61
  722.3 71.3 %all-to-all-done.5 = bf16[64,28,2048]{2,1,0:T(8,128)(2,1)} async-done(((bf16[64,28,2048]{2,1,0:T(8,128)(2,1)}), bf16[64,28,2048]{2,1,0:T(8,128)(2,1)}, u32[]{:S(2)}, u32[]{:S(2)}) %all-to-all-start.5) | async-done | bytes 7340064 | tf_op jit(solution)/shard_map/all_to_all | solution.py:44
  793.6 8.6 all-to-all-start.3
  802.3 10.6 %fusion.31 = bf16[1,768,2048]{2,1,0:T(8,128)(2,1)} fusion(bf16[1792,768]{1,0:T(8,128)(2,1)S(1)} %get-tuple-element.128, bf16[1792,2048]{1,0:T(8,128)(2,1)} %get-tuple-element.568), kind=kOutput, calls=%fused_computation.62 | convolution fusion | flops 5638717440 | bytes 13238272 | tf_op jit(solution)/shard_map/dot_general | solution.py:21
  813.1 5.1 reshape_bitcast_fusion
  818.2 8.3 copy.50
  826.5 5.2 reshape_bitcast_fusion.1
  831.7 8.2 copy.48
  839.9 10.2 %reshape.362 = bf16[1792,2048]{1,0:T(8,128)(2,1)} reshape(bf16[64,28,2048]{2,1,0:T(8,128)(2,1)} %all-to-all-done.5) | data formatting | bytes 14680064 | tf_op jit(solution)/shard_map/reshape | solution.py:185
  850.1 12.8 %gather_fusion.5 = bf16[1024,2048]{1,0:T(8,128)(2,1)} fusion(bf16[1792,2048]{1,0:T(8,128)(2,1)} %reshape.362, s32[1024]{0:T(1024)S(1)} %broadcast_clamp_fusion), kind=kCustom, calls=%fused_computation.5 | custom fusion | bytes 8392704 | tf_op jit(solution)/shard_map/gather | solution.py:186
  862.9 45.1 %all-to-all-done.3 = bf16[64,28,2048]{2,1,0:T(8,128)(2,1)} async-done(((bf16[64,28,2048]{2,1,0:T(8,128)(2,1)}), bf16[64,28,2048]{2,1,0:T(8,128)(2,1)}, u32[]{:S(2)}, u32[]{:S(2)}) %all-to-all-start.3) | async-done | bytes 7340064 | tf_op jit(solution)/shard_map/all_to_all | solution.py:44
  908.0 11.0 %reshape.358 = bf16[1792,2048]{1,0:T(8,128)(2,1)} reshape(bf16[64,28,2048]{2,1,0:T(8,128)(2,1)} %all-to-all-done.3) | data formatting | bytes 14680064 | tf_op jit(solution)/shard_map/reshape | solution.py:119
  919.0 13.1 %gather_fusion.2 = bf16[1024,2048]{1,0:T(8,128)(2,1)} fusion(bf16[1792,2048]{1,0:T(8,128)(2,1)} %reshape.358, s32[1024]{0:T(1024)S(1)} %broadcast_clamp_fusion), kind=kCustom, calls=%fused_computation.2 | custom fusion | bytes 8392704 | tf_op jit(solution)/shard_map/gather | solution.py:120
  932.1 3.6 fusion.21
  936.8 2.7 fusion.19
  940.2 5.9 bitcast_reduce_fusion
  (151 shorter events, 58.8 us)
Async XLA Ops:
  7.2 46.5 %copy-start = (bf16[128,2048]{1,0:T(8,128)(2,1)S(1)}, bf16[128,2048]{1,0:T(8,128)(2,1)}, u32[]{:S(2)}) copy-start(bf16[128,2048]{1,0:T(8,128)(2,1)} %param.11) | copy-start | bytes 1572868
  27.7 20.0 %all-to-all-start = ((bf16[64,1,1]{2,1,0:T(2,128)(2,1)}), bf16[64,1,1]{2,1,0:T(2,128)(2,1)S(1)}, u32[]{:S(2)}, u32[]{:S(2)}) async-start(bf16[64,1,1]{2,1,0:T(2,128)(2,1)} %copy.33), calls=%async_computation | async-start | bytes 65536 | tf_op jit(solution)/shard_map/all_to_all | solution.py:71
  40.8 45.8 %copy-start.10 = (s32[1024,1]{0,1:T(1,128)}, s32[1024,1]{0,1:T(1,128)S(1)}, u32[]{:S(2)}) copy-start(s32[1024,1]{0,1:T(1,128)S(1)} %compare_select_fusion.10) | copy-start | bytes 12292
  47.7 27.5 %all-to-all-start.1 = ((bf16[64,1,1]{2,1,0:T(2,128)(2,1)}), bf16[64,1,1]{2,1,0:T(2,128)(2,1)S(1)}, u32[]{:S(2)}, u32[]{:S(2)}) async-start(bf16[64,1,1]{2,1,0:T(2,128)(2,1)} %copy.35), calls=%async_computation.1 | async-start | bytes 65536 | tf_op jit(solution)/shard_map/all_to_all | solution.py:72
  75.2 11.0 %copy-start.6 = (bf16[128,2048]{1,0:T(8,128)(2,1)S(1)}, bf16[128,2048]{1,0:T(8,128)(2,1)}, u32[]{:S(2)}) copy-start(bf16[128,2048]{1,0:T(8,128)(2,1)} %param.14) | copy-start | bytes 1572868
  75.2 11.2 %copy-start.8 = (f32[128,8]{0,1:T(8,128)S(1)}, f32[128,8]{0,1:T(8,128)}, u32[]{:S(2)}) copy-start(f32[128,8]{0,1:T(8,128)} %param.13) | copy-start | bytes 12292
  75.2 123.6 %all-to-all-start.2 = ((bf16[64,28,2048]{2,1,0:T(8,128)(2,1)}), bf16[64,28,2048]{2,1,0:T(8,128)(2,1)}, u32[]{:S(2)}, u32[]{:S(2)}) async-start(bf16[64,28,2048]{2,1,0:T(8,128)(2,1)} %reshape.356), calls=%async_computation.2 | async-start | bytes 16777216 | tf_op jit(solution)/shard_map/all_to_all | solution.py:70
  198.8 114.4 %all-to-all-start.4 = ((bf16[64,28,2048]{2,1,0:T(8,128)(2,1)}), bf16[64,28,2048]{2,1,0:T(8,128)(2,1)}, u32[]{:S(2)}, u32[]{:S(2)}) async-start(bf16[64,28,2048]{2,1,0:T(8,128)(2,1)} %reshape.360), calls=%async_computation.4 | async-start | bytes 16777216 | tf_op jit(solution)/shard_map/all_to_all | solution.py:131
  208.8 604.4 %reduce-scatter.12.cloned.1.call-start = ((), (), s32[]{:S(2)}) async-start(), calls=%async_computation.11 | async-start | bytes 4718592
  362.9 3.6 copy-start.3
  362.9 6.0 copy-start.12
  370.2 3.5 copy-start.3
  370.2 5.9 copy-start.12
  377.6 3.5 copy-start.3
  377.6 5.9 copy-start.12
  384.9 3.5 copy-start.3
  384.9 5.9 copy-start.12
  392.2 3.5 copy-start.3
  392.2 5.9 copy-start.12
  399.6 3.5 copy-start.3
  399.6 5.9 copy-start.12
  414.4 4.3 copy-start.4
  414.4 5.5 copy-start.2
  421.9 4.4 copy-start.4
  421.9 5.5 copy-start.2
  429.3 4.3 copy-start.4
  429.3 5.5 copy-start.2
  436.8 4.4 copy-start.4
  436.8 5.5 copy-start.2
  444.4 4.4 copy-start.4
  444.4 5.5 copy-start.2
  451.8 4.3 copy-start.4
  451.8 5.5 copy-start.2
  562.3 231.4 %all-to-all-start.5 = ((bf16[64,28,2048]{2,1,0:T(8,128)(2,1)}), bf16[64,28,2048]{2,1,0:T(8,128)(2,1)}, u32[]{:S(2)}, u32[]{:S(2)}) async-start(bf16[64,28,2048]{2,1,0:T(8,128)(2,1)} %get-tuple-element.243), calls=%async_computation.5 | async-start | bytes 16777216 | tf_op jit(solution)/shard_map/all_to_all | solution.py:44
  689.8 136.7 %reduce-scatter.10.cloned.1.call-start = ((), (), s32[]{:S(2)}) async-start(), calls=%async_computation.10 | async-start | bytes 4718592
  793.6 114.4 %all-to-all-start.3 = ((bf16[64,28,2048]{2,1,0:T(8,128)(2,1)}), bf16[64,28,2048]{2,1,0:T(8,128)(2,1)}, u32[]{:S(2)}, u32[]{:S(2)}) async-start(bf16[64,28,2048]{2,1,0:T(8,128)(2,1)} %get-tuple-element.244), calls=%async_computation.3 | async-start | bytes 16777216 | tf_op jit(solution)/shard_map/all_to_all | solution.py:44
  802.2 143.9 %reduce-scatter.8.cloned.1.call-start = ((), (), s32[]{:S(2)}) async-start(), calls=%async_computation.9 | async-start | bytes 4718592 | tf_op jit(solution)/shard_map/reduce_scatter | solution.py:181
  802.2 10.7 %copy-start.9 = (f32[128,8]{0,1:T(8,128)S(1)}, f32[128,8]{0,1:T(8,128)}, u32[]{:S(2)}) copy-start(f32[128,8]{0,1:T(8,128)} %param.13) | copy-start | bytes 12292
  802.2 10.8 %copy-start.11 = (s32[1024,1]{0,1:T(1,128)S(1)}, s32[1024,1]{0,1:T(1,128)}, u32[]{:S(2)}) copy-start(s32[1024,1]{0,1:T(1,128)} %copy-done.10) | copy-start | bytes 12292
  932.1 4.7 copy-start.5
  932.1 4.7 copy-start.7
  936.8 9.3 copy-start.1
Sparse Core Ops, SparseCore 0:
  492.2 131.8 reduce-scatter.11
  722.5 14.8 reduce-scatter.9
  813.0 14.8 reduce-scatter.7
where the time goes:
time: 967 us; the launch traced here: 953 us
  local copies, waits for them, and re-layouts  294 us (30%)
  waiting for transfers between devices  241 us (25%)
  starting transfers between devices  175 us (18%)
  matrix products  126 us (13%)
  other arithmetic  101 us (10%)
  between operations  15.1 us (2%)
    all_to_all x2, starting transfers between devices, to_sources(): lax.all_to_all(returned, 'expert', split_axis=0, concat_axis=0, tiled=True)  136 us
    all_to_all x2, waiting for transfers between devices, to_sources(): lax.all_to_all(returned, 'expert', split_axis=0, concat_axis=0, tiled=True)  116 us
    all_to_all x1, waiting for transfers between devices, body(): lax.all_to_all(send_inputs, 'expert', split_axis=0, concat_axis=0, tiled=...  90.2 us
    unnamed x29, local copies, waits for them, and re-layouts  72.2 us
    gather x4, local copies, waits for them, and re-layouts, unpack(): rows_packed[unpack_at]  58.2 us
    dot_general x18, matrix products, contract_last(): lax.dot_general(left_side, right_side, (((1,), (1,)), ((), ())), preferre...  44.7 us
    gather x3, other arithmetic, pack_tables(): run_starts[source_of]  40.9 us
    dot_general x3, matrix products, contract_rows(): lax.dot_general(left_side, right_side, (((0,), (0,)), ((), ())), preferre...  31.2 us
  transfers between devices with their start and end apart: 9, of which 5 were waited for; matrix products, arithmetic and copies ran while one was open for 34% of the time, Pallas kernels for 0%

commit v1 on v0

v1 whole, which is shorter than its diff:
```python
import functools

import jax
import jax.numpy as jnp
from jax import lax
from jax.experimental import pallas as pl
from jax.experimental.pallas import tpu as pltpu
from jax.sharding import PartitionSpec as P

D = 2048
FF = 768
TOP = 8
TOK = 128
CAP = 28
SIDE = 4
EXPERTS = 64
GROUP = SIDE * CAP
ROWS = 16 * GROUP
WIDE = D + 128
HALF = 2
MESH = pl.DeviceIdType.MESH
VMEM_LIMIT = 60 * 1024 * 1024


def where_am_i():
    e = lax.axis_index("expert")
    return lax.axis_index("dp"), e // 16, (e // 4) % 4, e % 4


class Way:
    def __init__(self, t):
        self.t = t
        self.dp, z, self.x, y = where_am_i()
        self.a, self.b = (y, z) if t == 0 else (z, y)

    def dev(self, a, b, x):
        z, y = (b, a) if self.t == 0 else (a, b)
        return (self.dp, z * 16 + x * 4 + y)

    def block(self, a, b):
        return a * 4 + b if self.t == 0 else b * 4 + a


def step(v, d):
    return lax.rem(v + d + SIDE, SIDE)


def greet_lines():
    dp, z, x, y = where_am_i()
    barrier = pltpu.get_barrier_semaphore()
    for d in (1, 2, 3):
        for to in (
            step(z, d) * 16 + x * 4 + y,
            z * 16 + step(x, d) * 4 + y,
            z * 16 + x * 4 + step(y, d),
        ):
            pl.semaphore_signal(barrier, inc=1, device_id=(dp, to), device_id_type=MESH)
    pl.semaphore_wait(barrier, 9)


def remote(src, dst, send, recv, dev):
    return pltpu.make_async_remote_copy(
        src_ref=src, dst_ref=dst, send_sem=send, recv_sem=recv, device_id=dev, device_id_type=MESH
    )


def own_table(t, ids_ref, probs_ref):
    row = lax.broadcasted_iota(jnp.int32, (TOK, TOK), 0)
    b, x, kind, a = row // 32, (row // 8) % 4, (row // 4) % 2, row % 4
    expert = b * 16 + x * 4 + a if t == 0 else a * 16 + x * 4 + b
    hit = jnp.zeros((TOK, TOK), jnp.float32)
    weight = jnp.zeros((TOK, TOK), jnp.float32)
    for k in range(TOP):
        same = expert == ids_ref[k : k + 1, :]
        hit = jnp.where(same, 1.0, hit)
        weight = jnp.where(same, probs_ref[k : k + 1, :], weight)
    before = lax.broadcasted_iota(jnp.int32, (TOK, TOK), 0) < lax.broadcasted_iota(
        jnp.int32, (TOK, TOK), 1
    )
    before = jnp.where(before, 1.0, 0.0).astype(jnp.bfloat16)
    slot = jnp.dot(hit.astype(jnp.bfloat16), before, preferred_element_type=jnp.float32)
    slot = jnp.where(hit > 0.5, slot, -1000.0)
    return jnp.where(kind == 0, slot, weight)


def lane_rows(tables, kind, a):
    return [tables[xs, kind * 4 + a : kind * 4 + a + 1, :] for xs in range(SIDE)]


def hits_of(tables, a):
    slots = jnp.concatenate(
        [v + float(CAP * xs) for xs, v in enumerate(lane_rows(tables, 0, a))], axis=1
    )
    row = lax.broadcasted_iota(jnp.int32, (GROUP, SIDE * TOK), 0).astype(jnp.float32)
    return row == slots


def dispatch_kernel(
    ids_ref, probs_ref, tok_ref, cot_ref, x_rows, g_rows, tab_out,
    gath, stage, own_tab, tab_a, tab_b, pick, scale,
    s1, r1, s2, r2, s3, r3, ts1, tr1, ts2, tr2, ls,
):
    ways = (Way(0), Way(1))
    rows_out = (x_rows, g_rows)
    width = D // HALF

    for t, src in ((0, tok_ref), (1, cot_ref)):
        w = ways[t]
        own_tab[t] = own_table(t, ids_ref, probs_ref).reshape(16, 8, TOK)
        gath[t, w.b, w.x] = src[...]
        tab_a[t, w.b] = own_tab[t, pl.ds(w.b * 4, 4)]
    greet_lines()

    def first(t, d, h):
        w = ways[t]
        cols = pl.ds(h * width, width)
        ref = gath.at[t, w.b, w.x, :, cols]
        return remote(ref, ref, s1.at[t, d - 1, h], r1.at[t, d - 1, h],
                      w.dev(w.a, step(w.b, d), w.x))

    def first_tab(t, d):
        w = ways[t]
        to = step(w.b, d)
        return remote(own_tab.at[t, pl.ds(to * 4, 4)], tab_a.at[t, w.b],
                      ts1.at[t, d - 1], tr1.at[t, d - 1], w.dev(w.a, to, w.x))

    def second(t, kk, d, h):
        w = ways[t]
        bs = step(w.b, -kk)
        ref = gath.at[t, bs, w.x, :, pl.ds(h * width, width)]
        return remote(ref, ref, s2.at[t, kk, d - 1, h], r2.at[t, kk, d - 1, h],
                      w.dev(w.a, w.b, step(w.x, d)))

    def second_tab(t, kk, d):
        w = ways[t]
        bs = step(w.b, -kk)
        to = step(w.x, d)
        return remote(tab_a.at[t, bs, to], tab_b.at[t, bs, w.x],
                      ts2.at[t, kk, d - 1], tr2.at[t, kk, d - 1], w.dev(w.a, w.b, to))

    def third(t, kk, d, h):
        w = ways[t]
        bs = step(w.b, -kk)
        to = step(w.a, d)
        cols = pl.ds(h * width, width)
        return remote(stage.at[t, kk, to, :, cols],
                      rows_out[t].at[w.block(w.a, bs), :, cols],
                      s3.at[t, kk, d - 1, h], r3.at[t, kk, d - 1, h], w.dev(to, w.b, w.x))

    def kept(t, kk, h):
        w = ways[t]
        bs = step(w.b, -kk)
        cols = pl.ds(h * width, width)
        return pltpu.make_async_copy(stage.at[t, kk, w.a, :, cols],
                                     rows_out[t].at[w.block(w.a, bs), :, cols],
                                     ls.at[t, kk, h])

    def start_second(kk, h):
        for t in (0, 1):
            w = ways[t]
            bs = step(w.b, -kk)
            if kk > 0:
                first(t, kk, h).wait_recv()
                if h == 0:
                    first_tab(t, kk).wait_recv()
            if h == 0:
                tab_b[t, bs, w.x] = tab_a[t, bs, w.x]
                for d in (1, 2, 3):
                    second_tab(t, kk, d).start()
            for d in (1, 2, 3):
                second(t, kk, d, h).start()

    for t in (0, 1):
        for d in (1, 2, 3):
            first_tab(t, d).start()
    start_second(0, 0)
    for h in range(HALF):
        for t in (0, 1):
            for d in (1, 2, 3):
                first(t, d, h).start()

    turns = [(kk, h) for kk in range(SIDE) for h in range(HALF)]
    for n, (kk, h) in enumerate(turns):
        if n + 1 < len(turns):
            start_second(*turns[n + 1])
        for t in (0, 1):
            w = ways[t]
            bs = step(w.b, -kk)
            for d in (1, 2, 3):
                if h == 0:
                    second_tab(t, kk, d).wait_recv()
                second(t, kk, d, h).wait_recv()
            if h == 0:
                tables = tab_b[t, bs]
                for a in range(SIDE):
                    hit = hits_of(tables, a)
                    pick[t, a * GROUP : (a + 1) * GROUP, :] = jnp.where(hit, 1.0, 0.0).astype(
                        jnp.bfloat16
                    )
                    if t == 1:
                        weight = jnp.concatenate(lane_rows(tables, 1, a), axis=1)
                        weight = jnp.sum(jnp.where(hit, weight, 0.0), axis=1, keepdims=True)
                        scale[a * GROUP : (a + 1) * GROUP, :] = jnp.broadcast_to(
                            weight, (GROUP, 128)
                        )

            def tile(c, _, t=t, bs=bs, kk=kk, h=h):
                cols = pl.ds(pl.multiple_of(h * width + c * 256, 256), 256)
                block = gath[t, bs, :, :, cols].reshape(SIDE * TOK, 256)
                rows = jnp.dot(pick[t], block, preferred_element_type=jnp.float32)
                if t == 1:
                    rows = rows * jnp.concatenate([scale[...], scale[...]], axis=1)
                stage[t, kk, :, :, cols] = rows.astype(jnp.bfloat16).reshape(SIDE, GROUP, 256)
                return 0

            lax.fori_loop(0, width // 256, tile, 0)
            for d in (1, 2, 3):
                third(t, kk, d, h).start()
            kept(t, kk, h).start()

    tab_out[...] = tab_b[...]
    for t in (0, 1):
        for kk, h in turns:
            for d in (1, 2, 3):
                third(t, kk, d, h).wait()
                second(t, kk, d, h).wait_send()
                if h == 0:
                    second_tab(t, kk, d).wait_send()
            kept(t, kk, h).wait()
        for d in (1, 2, 3):
            first_tab(t, d).wait_send()
            for h in range(HALF):
                first(t, d, h).wait_send()


def dispatch(ids_t, probs_t, tokens, cotangent):
    dma = pltpu.SemaphoreType.DMA
    vmem = pl.BlockSpec(memory_space=pltpu.VMEM)
    hbm = pl.BlockSpec(memory_space=pl.ANY)
    return pl.pallas_call(
        dispatch_kernel,
        name="dispatch",
        out_shape=(
            jax.ShapeDtypeStruct((16, GROUP, D), jnp.bfloat16),
            jax.ShapeDtypeStruct((16, GROUP, D), jnp.bfloat16),
            jax.ShapeDtypeStruct((2, SIDE, SIDE, 8, TOK), jnp.float32),
        ),
        in_specs=[vmem] * 4,
        out_specs=(hbm, hbm, vmem),
        scratch_shapes=[
            pltpu.VMEM((2, SIDE, SIDE, TOK, D), jnp.bfloat16),
            pltpu.VMEM((2, SIDE, SIDE, GROUP, D), jnp.bfloat16),
            pltpu.VMEM((2, 16, 8, TOK), jnp.float32),
            pltpu.VMEM((2, SIDE, SIDE, 8, TOK), jnp.float32),
            pltpu.VMEM((2, SIDE, SIDE, 8, TOK), jnp.float32),
            pltpu.VMEM((2, SIDE * GROUP, SIDE * TOK), jnp.bfloat16),
            pltpu.VMEM((SIDE * GROUP, 128), jnp.float32),
            dma((2, 3, HALF)), dma((2, 3, HALF)),
            dma((2, SIDE, 3, HALF)), dma((2, SIDE, 3, HALF)),
            dma((2, SIDE, 3, HALF)), dma((2, SIDE, 3, HALF)),
            dma((2, 3)), dma((2, 3)),
            dma((2, SIDE, 3)), dma((2, SIDE, 3)),
            dma((2, SIDE, HALF)),
        ],
        compiler_params=pltpu.CompilerParams(
            collective_id=1, has_side_effects=True, vmem_limit_bytes=VMEM_LIMIT
        ),
    )(ids_t, probs_t, tokens, cotangent)


def contract_last(left_side, right_side):
    return lax.dot_general(
        left_side, right_side, (((1,), (1,)), ((), ())), preferred_element_type=jnp.float32
    )


def contract_rows(left_side, right_side):
    return lax.dot_general(
        left_side, right_side, (((0,), (0,)), ((), ())), preferred_element_type=jnp.float32
    )


def expert_kernel(x_ref, g_ref, wg_ref, wu_ref, wd_ref, out_ref, grad_ref, hid_ref, gg_ref, gu_ref):
    rows = x_ref[...]
    gate_pre = jnp.dot(rows, wg_ref[...], preferred_element_type=jnp.float32)
    up_pre = jnp.dot(rows, wu_ref[...], preferred_element_type=jnp.float32)
    sigmoid = jax.nn.sigmoid(gate_pre)
    activation = gate_pre * sigmoid
    derivative = sigmoid * (1.0 + gate_pre * (1.0 - sigmoid))
    hidden = (activation * up_pre).astype(jnp.bfloat16)
    hid_ref[...] = hidden
    out_ref[...] = jnp.dot(hidden, wd_ref[...], preferred_element_type=jnp.float32).astype(
        jnp.bfloat16
    )
    grad_hidden = contract_last(g_ref[...], wd_ref[...])
    gate_grad = (grad_hidden * up_pre * derivative).astype(jnp.bfloat16)
    up_grad = (grad_hidden * activation).astype(jnp.bfloat16)
    gg_ref[...] = gate_grad
    gu_ref[...] = up_grad
    grad_ref[:, :D] = (
        contract_last(gate_grad, wg_ref[...]) + contract_last(up_grad, wu_ref[...])
    ).astype(jnp.bfloat16)
    product = jnp.sum(hidden.astype(jnp.float32) * grad_hidden, axis=1, keepdims=True)
    high = product.astype(jnp.bfloat16)
    low = (product - high.astype(jnp.float32)).astype(jnp.bfloat16)
    lane = lax.broadcasted_iota(jnp.int32, (rows.shape[0], 128), 1)
    me = lax.axis_index("expert")
    marks = jnp.where(lane == me, high.astype(jnp.float32), 0.0)
    marks = jnp.where(lane == me + EXPERTS, low.astype(jnp.float32), marks)
    grad_ref[:, D:] = marks.astype(jnp.bfloat16)


def expert_rows(x_rows, g_rows, w_gate, w_up, w_down):
    bm = 256
    whole = lambda shape: pl.BlockSpec(shape, lambda i: (0, 0), pipeline_mode=pl.Buffered(1))
    part = lambda width: pl.BlockSpec((bm, width), lambda i: (i, 0))
    bf = lambda width: jax.ShapeDtypeStruct((ROWS, width), jnp.bfloat16)
    return pl.pallas_call(
        expert_kernel,
        name="expert_rows",
        grid=(ROWS // bm,),
        out_shape=(bf(D), bf(WIDE), bf(FF), bf(FF), bf(FF)),
        in_specs=[part(D), part(D), whole((D, FF)), whole((D, FF)), whole((FF, D))],
        out_specs=(part(D), part(WIDE), part(FF), part(FF), part(FF)),
        compiler_params=pltpu.CompilerParams(vmem_limit_bytes=VMEM_LIMIT),
        cost_estimate=pl.CostEstimate(
            flops=12 * ROWS * D * FF, bytes_accessed=40_000_000, transcendentals=ROWS * FF
        ),
    )(x_rows, g_rows, w_gate, w_up, w_down)


def weight_kernel(x_ref, g_ref, hid_ref, gg_ref, gu_ref, dg_ref, du_ref, dd_ref,
                  out_g, out_u, out_d, in_g, in_u, in_d, send, recv):
    dp = lax.axis_index("dp")
    e = lax.axis_index("expert")
    other = 1 - dp
    barrier = pltpu.get_barrier_semaphore()
    pl.semaphore_signal(barrier, inc=1, device_id=(other, e), device_id_type=MESH)
    pl.semaphore_wait(barrier, 1)
    jobs = (
        (x_ref, gg_ref, dg_ref, out_g, in_g),
        (x_ref, gu_ref, du_ref, out_u, in_u),
        (hid_ref, g_ref, dd_ref, out_d, in_d),
    )
    copies = []
    for n, (left, right, done, away, back) in enumerate(jobs):
        height = 256
        wide = right.shape[1] // 2

        def send_part(i, _, left=left, right=right, away=away, wide=wide):
            at = pl.ds(pl.multiple_of(i * height, height), height)
            cols = pl.ds(pl.multiple_of(other * wide, wide), wide)
            away[at, :] = contract_rows(left[:, at], right[:, cols]).astype(jnp.bfloat16)
            return 0

        lax.fori_loop(0, left.shape[1] // height, send_part, 0)
        copy = remote(away, back, send.at[n], recv.at[n], (other, e))
        copy.start()
        copies.append(copy)
    for n, (left, right, done, away, back) in enumerate(jobs):
        height = 256
        wide = right.shape[1] // 2
        copies[n].wait()

        def keep_part(i, _, left=left, right=right, back=back, done=done, wide=wide):
            at = pl.ds(pl.multiple_of(i * height, height), height)
            cols = pl.ds(pl.multiple_of(dp * wide, wide), wide)
            mine = contract_rows(left[:, at], right[:, cols])
            done[0, at, :] = (mine + back[at, :].astype(jnp.float32)).astype(jnp.bfloat16)
            return 0

        lax.fori_loop(0, left.shape[1] // height, keep_part, 0)


def weight_grads(x_rows, g_rows, hidden, gate_grad, up_grad):
    vmem = pl.BlockSpec(memory_space=pltpu.VMEM)
    halves = ((D, FF // 2), (D, FF // 2), (FF, D // 2))
    dma = pltpu.SemaphoreType.DMA
    return pl.pallas_call(
        weight_kernel,
        name="weight_grads",
        out_shape=tuple(jax.ShapeDtypeStruct((1,) + s, jnp.bfloat16) for s in halves),
        in_specs=[vmem] * 5,
        out_specs=(vmem,) * 3,
        scratch_shapes=[pltpu.VMEM(s, jnp.bfloat16) for s in halves + halves] + [dma((3,)), dma((3,))],
        compiler_params=pltpu.CompilerParams(
            collective_id=2, has_side_effects=True, vmem_limit_bytes=VMEM_LIMIT
        ),
    )(x_rows, g_rows, hidden, gate_grad, up_grad)


def return_kernel(
    out_rows, grad_rows, tab_ref, mixed_ref, gtok_ref, mark_ref,
    back0, back1, part0, part1, across0, across1, zs0, zs1, zb0, zb1, pick,
    sa, ra, sb, rb, sc, rc, la,
):
    ways = (Way(0), Way(1))
    rows_in = (out_rows, grad_rows)
    back, part, across = (back0, back1), (part0, part1), (across0, across1)
    zs, zb = (zs0, zs1), (zb0, zb1)
    wides = (D, WIDE)
    order = (1, 2, 3, 0)
    greet_lines()

    def home(t, kk, d):
        w = ways[t]
        bs = step(w.b, kk)
        to = step(w.a, d)
        return remote(rows_in[t].at[w.block(to, bs)], back[t].at[bs, w.a],
                      sa.at[t, kk, d - 1], ra.at[t, kk, d - 1], w.dev(to, w.b, w.x))

    def stay(t, kk):
        w = ways[t]
        bs = step(w.b, kk)
        return pltpu.make_async_copy(rows_in[t].at[w.block(w.a, bs)], back[t].at[bs, w.a],
                                     la.at[t, kk])

    def cross(t, n, kk, d):
        w = ways[t]
        bs = step(w.b, kk)
        to = step(w.x, d)
        return remote(part[t].at[n % 2, to], across[t].at[bs, w.x],
                      sb.at[t, kk, d - 1], rb.at[t, kk, d - 1], w.dev(w.a, w.b, to))

    def last(t, kk):
        w = ways[t]
        return remote(zs[t].at[kk - 1], zb[t].at[kk - 1], sc.at[t, kk - 1], rc.at[t, kk - 1],
                      w.dev(w.a, step(w.b, kk), w.x))

    for kk in order:
        for t in (0, 1):
            for d in (1, 2, 3):
                home(t, kk, d).start()
            stay(t, kk).start()

    def gather_x(t, kk):
        w = ways[t]
        bs = step(w.b, kk)
        for d in (1, 2, 3):
            cross(t, 0, kk, d).wait_recv()
        if kk == 0:
            return

        def total(c, _):
            cols = pl.ds(pl.multiple_of(c * 128, 128), 128)
            four = across[t][bs, :, :, cols].astype(jnp.float32)
            zs[t][kk - 1, :, cols] = jnp.sum(four, axis=0).astype(jnp.bfloat16)
            return 0

        lax.fori_loop(0, wides[t] // 128, total, 0)
        last(t, kk).start()

    for n, kk in enumerate(order):
        for t in (0, 1):
            w = ways[t]
            bs = step(w.b, kk)
            tables = tab_ref[t, bs]
            for a in range(SIDE):
                hit = hits_of(tables, a)
                weight = jnp.concatenate(lane_rows(tables, 1, a), axis=1) if t == 0 else 1.0
                pick[a * GROUP : (a + 1) * GROUP, :] = jnp.where(hit, weight, 0.0).astype(
                    jnp.bfloat16
                )
            for d in (1, 2, 3):
                home(t, kk, d).wait_recv()
            stay(t, kk).wait()
            if n >= 2:
                for d in (1, 2, 3):
                    cross(t, n - 2, order[n - 2], d).wait_send()

            def dense(c, _, t=t, bs=bs, n=n):
                cols = pl.ds(pl.multiple_of(c * 128, 128), 128)
                rows = back[t][bs, :, :, cols].reshape(SIDE * GROUP, 128)
                sums = contract_rows(pick[...], rows).astype(jnp.bfloat16)
                part[t][n % 2, :, :, cols] = sums.reshape(SIDE, TOK, 128)
                return 0

            lax.fori_loop(0, wides[t] // 128, dense, 0)
            for d in (1, 2, 3):
                cross(t, n, kk, d).start()
            across[t][bs, w.x] = part[t][n % 2, w.x]
        if n >= 1:
            for t in (0, 1):
                gather_x(t, order[n - 1])
    for t in (0, 1):
        gather_x(t, 0)
        for kk in (1, 2, 3):
            last(t, kk).wait_recv()
        w = ways[t]

        def finish(c, _, t=t, w=w):
            cols = pl.ds(pl.multiple_of(c * 128, 128), 128)
            four = jnp.sum(across[t][w.b, :, :, cols].astype(jnp.float32), axis=0)
            rest = jnp.sum(zb[t][:, :, cols].astype(jnp.float32), axis=0)
            (mixed_ref, gtok_ref)[t][:, cols] = (four + rest).astype(jnp.bfloat16)
            return 0

        lax.fori_loop(0, D // 128, finish, 0)
        if t == 1:
            marks = jnp.sum(across[1][w.b, :, :, D:].astype(jnp.float32), axis=0)
            mark_ref[...] = marks + jnp.sum(zb[1][:, :, D:].astype(jnp.float32), axis=0)
    for t in (0, 1):
        for n, kk in enumerate(order):
            for d in (1, 2, 3):
                home(t, kk, d).wait_send()
                if n >= 2:
                    cross(t, n, kk, d).wait_send()
            if kk > 0:
                last(t, kk).wait_send()


def bring_back(out_rows, grad_rows, tables):
    dma = pltpu.SemaphoreType.DMA
    vmem = pl.BlockSpec(memory_space=pltpu.VMEM)
    hbm = pl.BlockSpec(memory_space=pl.ANY)
    both = lambda lead: [pltpu.VMEM(lead + (w,), jnp.bfloat16) for w in (D, WIDE)]
    return pl.pallas_call(
        return_kernel,
        name="bring_back",
        out_shape=(
            jax.ShapeDtypeStruct((TOK, D), jnp.bfloat16),
            jax.ShapeDtypeStruct((TOK, D), jnp.bfloat16),
            jax.ShapeDtypeStruct((TOK, 128), jnp.float32),
        ),
        in_specs=[hbm, hbm, vmem],
        out_specs=(vmem, vmem, vmem),
        scratch_shapes=both((SIDE, SIDE, GROUP)) + both((2, SIDE, TOK)) + both((SIDE, SIDE, TOK))
        + both((3, TOK)) + both((3, TOK)) + [
            pltpu.VMEM((SIDE * GROUP, SIDE * TOK), jnp.bfloat16),
            dma((2, SIDE, 3)), dma((2, SIDE, 3)),
            dma((2, SIDE, 3)), dma((2, SIDE, 3)),
            dma((2, 3)), dma((2, 3)),
            dma((2, SIDE)),
        ],
        compiler_params=pltpu.CompilerParams(
            collective_id=3, has_side_effects=True, vmem_limit_bytes=VMEM_LIMIT
        ),
    )(out_rows, grad_rows, tables)


def body(tokens, route_ids, route_probs, cotangent, w_gate, w_up, w_down):
    x_rows, g_rows, tables = dispatch(route_ids.T, route_probs.T, tokens, cotangent)
    x_rows, g_rows = x_rows.reshape(ROWS, D), g_rows.reshape(ROWS, D)
    out_rows, grad_rows, hidden, gate_grad, up_grad = expert_rows(
        x_rows, g_rows, w_gate[0], w_up[0], w_down[0]
    )
    mixed, grad_tokens, marks = bring_back(
        out_rows.reshape(16, GROUP, D), grad_rows.reshape(16, GROUP, WIDE), tables
    )
    grad_gate, grad_up, grad_down = weight_grads(x_rows, g_rows, hidden, gate_grad, up_grad)
    product = marks[:, :EXPERTS] + marks[:, EXPERTS:]
    chosen = route_ids[:, :, None] == jnp.arange(EXPERTS, dtype=jnp.int32)[None, None, :]
    grad_probs = jnp.sum(jnp.where(chosen, product[:, None, :], 0.0), axis=2) / route_probs
    return (mixed, grad_tokens, grad_probs, grad_gate, grad_up, grad_down)


def solution(mesh):
    both = P(("dp", "expert"), None)
    mine = P("expert", None, None)
    split = P("expert", None, "dp")
    return jax.shard_map(
        body,
        mesh=mesh,
        in_specs=(both, both, both, both, mine, mine, mine),
        out_specs=(both, both, both, split, split, split),
        check_vma=False,
    )
```

time: 967 us -> 524 us (0.54); the launches traced: 953 us -> 520 us
  Pallas kernels: 0 us -> 510 us
  local copies, waits for them, and re-layouts: 294 us -> 6.8 us
  waiting for transfers between devices: 241 us -> 0 us
  starting transfers between devices: 175 us -> 0 us
  matrix products: 126 us -> 0 us
  other arithmetic: 101 us -> 1.63 us
  between operations: 15.1 us -> 0.72 us
    pallas_call x0 -> x4, Pallas kernels: none -> 510 us  [the longest x1 219 us: bring_back(): pl.pallas_call(return_kernel, name='bring_back', out_shape=(jax.ShapeDtyp...]
    all_to_all x6 -> x0, waiting for transfers between devices: 241 us -> none  [the longest x2 116 us: to_sources(): lax.all_to_all(returned, 'expert', split_axis=0, concat_axis=0, tiled=True)]
    all_to_all x6 -> x0, starting transfers between devices: 175 us -> none  [the longest x2 136 us: to_sources(): lax.all_to_all(returned, 'expert', split_axis=0, concat_axis=0, tiled=True)]
    dot_general x41 -> x0, matrix products: 126 us -> none  [the longest x18 44.7 us: contract_last(): lax.dot_general(left_side, right_side, (((1,), (1,)), ((), ())), preferre...]
    gather x12 -> x0, local copies, waits for them, and re-layouts: 124 us -> none  [the longest x4 58.2 us: unpack(): rows_packed[unpack_at]]
    unnamed x29 -> x17, local copies, waits for them, and re-layouts: 72.2 us -> 6.74 us
    reshape x6 -> x0, local copies, waits for them, and re-layouts: 64.7 us -> none  [the longest x2 21.6 us: to_slots(): return placed.reshape(expert_count, capacity_slots, features)]
    gather x6 -> x0, other arithmetic: 40.9 us -> none  [the longest x3 40.9 us: pack_tables(): run_starts[source_of]]
  transfers between devices with their start and end apart: 9 -> 0, of which waited for: 5 -> 0; matrix products, arithmetic and copies ran while one was open for 34% -> 0% of each run, Pallas kernels for 0% -> 0%
where the time goes in v1:
time: 524 us; the launch traced here: 520 us
  Pallas kernels  510 us (97%)
  local copies, waits for them, and re-layouts  6.8 us (1%)
    pallas_call x1, Pallas kernels, bring_back(): pl.pallas_call(return_kernel, name='bring_back', out_shape=(jax.ShapeDtyp...  219 us
    pallas_call x1, Pallas kernels, dispatch(): pl.pallas_call(dispatch_kernel, name='dispatch', out_shape=(jax.ShapeDtyp...  207 us
    pallas_call x1, Pallas kernels, expert_rows(): pl.pallas_call(expert_kernel, name='expert_rows', grid=(ROWS // bm,), out...  46.9 us
    pallas_call x1, Pallas kernels, weight_grads(): pl.pallas_call(weight_kernel, name='weight_grads', out_shape=tuple((jax.S...  37.9 us

profile of v1, /device:TPU:2, one launch (start us, length us, event | category | flops | bytes accessed | tf_op | source)
XLA Modules:
  0.0 519.6 jit_solution(12830246752907500459)
XLA Ops:
  0.6 206.6 %dispatch.1 = (bf16[16,112,2048]{2,1,0:T(8,128)(2,1)}, bf16[16,112,2048]{2,1,0:T(8,128)(2,1)}, f32[2,4,4,8,128]{4,3,2,1,0:T(8,128)}) custom-call(s32[8,128]{1,0:T(8,128)} %bitcast.15, f32[8,128]{1,0:T(8,128)} %bitcast.16, bf16[128,2048]{1,0:T(8,128)(2,1)} %tok_ref.1, bf16[128,2048]{1,0:T(8,128)(2,1)} %cot_ref.1), custom_call_target="tpu_custom_call" | custom-call | tf_op jit(solution)/shard_map/dispatch/pallas_call | solution.py:240
  207.2 46.9 %expert_rows.1 = (bf16[1792,2048]{1,0:T(8,128)(2,1)}, bf16[1792,2176]{1,0:T(8,128)(2,1)}, bf16[1792,768]{1,0:T(8,128)(2,1)}, bf16[1792,768]{1,0:T(8,128)(2,1)}, bf16[1792,768]{1,0:T(8,128)(2,1)}) custom-call(bf16[1792,2048]{1,0:T(8,128)(2,1)} %bitcast.10, bf16[1792,2048]{1,0:T(8,128)(2,1)} %bitcast.12, bf16[2048,768]{1,0:T(8,128)(2,1)} %bitcast.17, ...), custom_call_target="tpu_custom_call" | custom-call | flops 33822867456 | bytes 40000000 | tf_op jit(solution)/shard_map/expert_rows/pallas_call | solution.py:318
  254.2 0.0 copy-start.4
  254.2 0.0 copy-start.5
  254.2 219.0 %bring_back.1 = (bf16[128,2048]{1,0:T(8,128)(2,1)}, bf16[128,2048]{1,0:T(8,128)(2,1)}, f32[128,128]{1,0:T(8,128)}) custom-call(bf16[16,112,2048]{2,1,0:T(8,128)(2,1)} %bitcast.14, bf16[16,112,2176]{2,1,0:T(8,128)(2,1)} %bitcast.9, f32[2,4,4,8,128]{4,3,2,1,0:T(8,128)} %get-tuple-element.24.tab_ref), custom_call_target="tpu_custom_call" | custom-call | tf_op jit(solution)/shard_map/bring_back/pallas_call | solution.py:517
  473.2 1.0 slice_add_fusion
  474.2 0.1 copy.14
  474.2 0.0 copy-done.4
  474.3 0.0 copy-done.5
  474.3 0.6 div.3
  474.9 0.0 copy-start.3
  474.9 0.0 copy-start.2
  474.9 37.9 %weight_grads.1 = (bf16[1,2048,384]{2,1,0:T(8,128)(2,1)}, bf16[1,2048,384]{2,1,0:T(8,128)(2,1)}, bf16[1,768,1024]{2,1,0:T(8,128)(2,1)}) custom-call(bf16[1792,2048]{1,0:T(8,128)(2,1)} %bitcast.11, bf16[1792,2048]{1,0:T(8,128)(2,1)} %bitcast.13, bf16[1792,768]{1,0:T(8,128)(2,1)} %get-tuple-element.28.hid_ref, bf16[1792,768]{1,0:T(8,128)(2,1)} %get-tuple-element.29.gg_ref, ...), custom_call_target="tpu_custom_call" | custom-call | tf_op jit(solution)/shard_map/weight_grads/pallas_call | solution.py:379
  512.8 0.0 copy-start.1
  512.9 0.0 copy-done.3
  512.9 0.8 copy.20
  513.7 0.0 copy-done.2
  513.7 0.8 copy.21
  514.5 0.0 copy-start
  514.5 2.8 copy.22
  517.3 0.0 copy-done.1
  517.3 1.1 copy.23
  518.4 0.0 copy-done
  518.4 1.1 copy.24
  (1 shorter events, 0.0 us)
Async XLA Ops:
  254.2 220.1 %copy-start.4 = (s32[128,8]{0,1:T(8,128)S(1)}, s32[128,8]{0,1:T(8,128)}, u32[]{:S(2)}) copy-start(s32[128,8]{0,1:T(8,128)} %param.8) | copy-start | bytes 12292
  254.2 220.1 %copy-start.5 = (f32[128,8]{0,1:T(8,128)S(1)}, f32[128,8]{0,1:T(8,128)}, u32[]{:S(2)}) copy-start(f32[128,8]{0,1:T(8,128)} %param.9) | copy-start | bytes 12292
  474.9 37.9 %copy-start.3 = (bf16[128,2048]{1,0:T(8,128)(2,1)S(1)}, bf16[128,2048]{1,0:T(8,128)(2,1)}, u32[]{:S(2)}) copy-start(bf16[128,2048]{1,0:T(8,128)(2,1)} %get-tuple-element.40) | copy-start | bytes 1572868
  474.9 38.8 %copy-start.2 = (bf16[128,2048]{1,0:T(8,128)(2,1)S(1)}, bf16[128,2048]{1,0:T(8,128)(2,1)}, u32[]{:S(2)}) copy-start(bf16[128,2048]{1,0:T(8,128)(2,1)} %get-tuple-element.41) | copy-start | bytes 1572868
  512.8 4.4 copy-start.1
  514.5 4.0 copy-start

commit v2 on v1

--- a/solution.py
+++ b/solution.py
@@ -17,7 +17,9 @@
 GROUP = SIDE * CAP
 ROWS = 16 * GROUP
 WIDE = D + 128
-HALF = 2
+LATE = 1536
+PIECES = ((0, 768), (768, 768), (1536, 512))
+RINGS = 24
 MESH = pl.DeviceIdType.MESH
 VMEM_LIMIT = 60 * 1024 * 1024
 
@@ -95,14 +97,58 @@
     return row == slots
 
 
+class Gather:
+    def __init__(self, n, sems, me, dev, block, half):
+        self.send, self.recv = sems
+        self.n, self.me, self.dev, self.block, self.half = n, me, dev, block, half
+
+    def copy(self, ref, at, s):
+        return remote(ref, ref, self.send.at[self.n, at], self.recv.at[self.n, at],
+                      self.dev(step(self.me, s)))
+
+    def near(self, s):
+        return self.copy(self.block(self.me), 0 if s > 0 else 1, s)
+
+    def far(self, s):
+        return self.copy(self.half(step(self.me, -s), 0 if s > 0 else 1), 2 if s > 0 else 3, s)
+
+    def start(self):
+        for s in (1, -1):
+            self.near(s).start()
+
+    def pass_on(self):
+        for s in (1, -1):
+            self.near(s).wait_recv()
+            self.far(s).start()
+
+    def finish(self):
+        for s in (1, -1):
+            self.far(s).wait_recv()
+
+    def drain(self):
+        for s in (1, -1):
+            self.near(s).wait_send()
+            self.far(s).wait_send()
+
+
+def column_tiles(start, width, tile):
+    def one(c, _):
+        tile(pl.ds(pl.multiple_of(start + c * 256, 128), 256))
+        return 0
+
+    lax.fori_loop(0, width // 256, one, 0)
+    if width % 256:
+        tile(pl.ds(start + width // 256 * 256, width % 256))
+
+
 def dispatch_kernel(
     ids_ref, probs_ref, tok_ref, cot_ref, x_rows, g_rows, tab_out,
     gath, stage, own_tab, tab_a, tab_b, pick, scale,
-    s1, r1, s2, r2, s3, r3, ts1, tr1, ts2, tr2, ls,
+    gs, gr, s3, r3, ts1, tr1, ts2, tr2, ls,
 ):
     ways = (Way(0), Way(1))
     rows_out = (x_rows, g_rows)
-    width = D // HALF
+    sems = (gs, gr)
 
     for t, src in ((0, tok_ref), (1, cot_ref)):
         w = ways[t]
@@ -111,25 +157,38 @@
         tab_a[t, w.b] = own_tab[t, pl.ds(w.b * 4, 4)]
     greet_lines()
 
-    def first(t, d, h):
-        w = ways[t]
-        cols = pl.ds(h * width, width)
-        ref = gath.at[t, w.b, w.x, :, cols]
-        return remote(ref, ref, s1.at[t, d - 1, h], r1.at[t, d - 1, h],
-                      w.dev(w.a, step(w.b, d), w.x))
+    count = iter(range(RINGS))
+
+    def along_b(t, piece):
+        w, cols = ways[t], pl.ds(*PIECES[piece])
+        return Gather(next(count), sems, w.b, lambda i: w.dev(w.a, i, w.x),
+                      lambda i: gath.at[t, i, w.x, :, cols],
+                      lambda i, u: gath.at[t, i, w.x, pl.ds(u * 64, 64), cols])
+
+    def along_x(t, kk, piece):
+        w, cols = ways[t], pl.ds(*PIECES[piece])
+        bs = step(w.b, -kk)
+        return Gather(next(count), sems, w.x, lambda i: w.dev(w.a, w.b, i),
+                      lambda i: gath.at[t, bs, i, :, cols],
+                      lambda i, u: gath.at[t, bs, i, pl.ds(u * 64, 64), cols])
+
+    def lines_b(t):
+        w, cols = ways[t], pl.ds(*PIECES[2])
+        return Gather(next(count), sems, w.b, lambda i: w.dev(w.a, i, w.x),
+                      lambda i: gath.at[t, i, :, :, cols],
+                      lambda i, u: gath.at[t, i, pl.ds(u * 2, 2), :, cols])
+
+    both = (0, 1)
+    b_first = [[along_b(t, h) for h in both] for t in both]
+    x_then = [{(kk, h): along_x(t, kk, h) for kk in range(SIDE) for h in both} for t in both]
+    x_first = [along_x(t, 0, 2) for t in both]
+    b_then = [lines_b(t) for t in both]
 
     def first_tab(t, d):
         w = ways[t]
         to = step(w.b, d)
         return remote(own_tab.at[t, pl.ds(to * 4, 4)], tab_a.at[t, w.b],
                       ts1.at[t, d - 1], tr1.at[t, d - 1], w.dev(w.a, to, w.x))
-
-    def second(t, kk, d, h):
-        w = ways[t]
-        bs = step(w.b, -kk)
-        ref = gath.at[t, bs, w.x, :, pl.ds(h * width, width)]
-        return remote(ref, ref, s2.at[t, kk, d - 1, h], r2.at[t, kk, d - 1, h],
-                      w.dev(w.a, w.b, step(w.x, d)))
 
     def second_tab(t, kk, d):
         w = ways[t]
@@ -138,99 +197,122 @@
         return remote(tab_a.at[t, bs, to], tab_b.at[t, bs, w.x],
                       ts2.at[t, kk, d - 1], tr2.at[t, kk, d - 1], w.dev(w.a, w.b, to))
 
-    def third(t, kk, d, h):
+    def third(t, kk, piece, d):
         w = ways[t]
         bs = step(w.b, -kk)
         to = step(w.a, d)
-        cols = pl.ds(h * width, width)
+        cols = pl.ds(*PIECES[piece])
         return remote(stage.at[t, kk, to, :, cols],
                       rows_out[t].at[w.block(w.a, bs), :, cols],
-                      s3.at[t, kk, d - 1, h], r3.at[t, kk, d - 1, h], w.dev(to, w.b, w.x))
-
-    def kept(t, kk, h):
+                      s3.at[t, kk, piece, d - 1], r3.at[t, kk, piece, d - 1],
+                      w.dev(to, w.b, w.x))
+
+    def kept(t, kk, piece):
         w = ways[t]
         bs = step(w.b, -kk)
-        cols = pl.ds(h * width, width)
+        cols = pl.ds(*PIECES[piece])
         return pltpu.make_async_copy(stage.at[t, kk, w.a, :, cols],
                                      rows_out[t].at[w.block(w.a, bs), :, cols],
-                                     ls.at[t, kk, h])
-
-    def start_second(kk, h):
-        for t in (0, 1):
-            w = ways[t]
-            bs = step(w.b, -kk)
-            if kk > 0:
-                first(t, kk, h).wait_recv()
-                if h == 0:
-                    first_tab(t, kk).wait_recv()
-            if h == 0:
-                tab_b[t, bs, w.x] = tab_a[t, bs, w.x]
-                for d in (1, 2, 3):
-                    second_tab(t, kk, d).start()
-            for d in (1, 2, 3):
-                second(t, kk, d, h).start()
-
-    for t in (0, 1):
+                                     ls.at[t, kk, piece])
+
+    def share_tab(t, kk):
+        w = ways[t]
+        bs = step(w.b, -kk)
+        if kk > 0:
+            first_tab(t, kk).wait_recv()
+        tab_b[t, bs, w.x] = tab_a[t, bs, w.x]
+        for d in (1, 2, 3):
+            second_tab(t, kk, d).start()
+
+    def make_pick(t, kk):
+        for d in (1, 2, 3):
+            second_tab(t, kk, d).wait_recv()
+        tables = tab_b[t, step(ways[t].b, -kk)]
+        for a in range(SIDE):
+            at = slice(a * GROUP, (a + 1) * GROUP)
+            hit = hits_of(tables, a)
+            pick[t, at, :] = jnp.where(hit, 1.0, 0.0).astype(jnp.bfloat16)
+            if t == 1:
+                weight = jnp.concatenate(lane_rows(tables, 1, a), axis=1)
+                weight = jnp.sum(jnp.where(hit, weight, 0.0), axis=1, keepdims=True)
+                scale[at, :] = jnp.broadcast_to(weight, (GROUP, 128))
+
+    def send_rows(t, kk, piece):
+        bs = step(ways[t].b, -kk)
+
+        def tile(cols):
+            block = gath[t, bs, :, :, cols].reshape(SIDE * TOK, cols.size)
+            rows = jnp.dot(pick[t], block, preferred_element_type=jnp.float32)
+            if t == 1:
+                rows = rows * jnp.concatenate([scale[...]] * (cols.size // 128), axis=1)
+            stage[t, kk, :, :, cols] = rows.astype(jnp.bfloat16).reshape(SIDE, GROUP, cols.size)
+
+        column_tiles(*PIECES[piece], tile)
+        for d in (1, 2, 3):
+            third(t, kk, piece, d).start()
+        kept(t, kk, piece).start()
+
+    for t in both:
         for d in (1, 2, 3):
             first_tab(t, d).start()
-    start_second(0, 0)
-    for h in range(HALF):
-        for t in (0, 1):
+        share_tab(t, 0)
+        x_first[t].start()
+    for h in both:
+        for t in both:
+            x_then[t][0, h].start()
+        for t in both:
+            b_first[t][h].start()
+    for t in both:
+        x_first[t].pass_on()
+    for t in both:
+        x_then[t][0, 0].pass_on()
+    for t in both:
+        b_first[t][0].pass_on()
+    for t in both:
+        x_first[t].finish()
+        b_then[t].start()
+    for t in both:
+        b_first[t][1].pass_on()
+
+    turns = [(kk, h) for kk in (0, 1, 3, 2) for h in both]
+    for n, (kk, h) in enumerate(turns):
+        if n + 2 < len(turns):
+            k2, h2 = turns[n + 2]
+            for t in both:
+                if k2 == 2:
+                    b_first[t][h2].finish()
+                if h2 == 0:
+                    share_tab(t, k2)
+                x_then[t][k2, h2].start()
+        if n + 1 < len(turns):
+            for t in both:
+                x_then[t][turns[n + 1]].pass_on()
+        for t in both:
+            x_then[t][kk, h].finish()
+            if h == 0:
+                make_pick(t, kk)
+            send_rows(t, kk, h)
+        if h == 1:
+            for t in both:
+                if kk == 1:
+                    b_then[t].pass_on()
+                if kk == 2:
+                    b_then[t].finish()
+                send_rows(t, kk, 2)
+
+    tab_out[...] = tab_b[...]
+    for t in both:
+        for kk in range(SIDE):
             for d in (1, 2, 3):
-                first(t, d, h).start()
-
-    turns = [(kk, h) for kk in range(SIDE) for h in range(HALF)]
-    for n, (kk, h) in enumerate(turns):
-        if n + 1 < len(turns):
-            start_second(*turns[n + 1])
-        for t in (0, 1):
-            w = ways[t]
-            bs = step(w.b, -kk)
-            for d in (1, 2, 3):
-                if h == 0:
-                    second_tab(t, kk, d).wait_recv()
-                second(t, kk, d, h).wait_recv()
-            if h == 0:
-                tables = tab_b[t, bs]
-                for a in range(SIDE):
-                    hit = hits_of(tables, a)
-                    pick[t, a * GROUP : (a + 1) * GROUP, :] = jnp.where(hit, 1.0, 0.0).astype(
-                        jnp.bfloat16
-                    )
-                    if t == 1:
-                        weight = jnp.concatenate(lane_rows(tables, 1, a), axis=1)
-                        weight = jnp.sum(jnp.where(hit, weight, 0.0), axis=1, keepdims=True)
-                        scale[a * GROUP : (a + 1) * GROUP, :] = jnp.broadcast_to(
-                            weight, (GROUP, 128)
-                        )
-
-            def tile(c, _, t=t, bs=bs, kk=kk, h=h):
-                cols = pl.ds(pl.multiple_of(h * width + c * 256, 256), 256)
-                block = gath[t, bs, :, :, cols].reshape(SIDE * TOK, 256)
-                rows = jnp.dot(pick[t], block, preferred_element_type=jnp.float32)
-                if t == 1:
-                    rows = rows * jnp.concatenate([scale[...], scale[...]], axis=1)
-                stage[t, kk, :, :, cols] = rows.astype(jnp.bfloat16).reshape(SIDE, GROUP, 256)
-                return 0
-
-            lax.fori_loop(0, width // 256, tile, 0)
-            for d in (1, 2, 3):
-                third(t, kk, d, h).start()
-            kept(t, kk, h).start()
-
-    tab_out[...] = tab_b[...]
-    for t in (0, 1):
-        for kk, h in turns:
-            for d in (1, 2, 3):
-                third(t, kk, d, h).wait()
-                second(t, kk, d, h).wait_send()
-                if h == 0:
-                    second_tab(t, kk, d).wait_send()
-            kept(t, kk, h).wait()
+                second_tab(t, kk, d).wait_send()
+                for piece in range(3):
+                    third(t, kk, piece, d).wait()
+            for piece in range(3):
+                kept(t, kk, piece).wait()
         for d in (1, 2, 3):
             first_tab(t, d).wait_send()
-            for h in range(HALF):
-                first(t, d, h).wait_send()
+        for ring in (*b_first[t], *x_then[t].values(), x_first[t], b_then[t]):
+            ring.drain()
 
 
 def dispatch(ids_t, probs_t, tokens, cotangent):
@@ -255,12 +337,11 @@
             pltpu.VMEM((2, SIDE, SIDE, 8, TOK), jnp.float32),
             pltpu.VMEM((2, SIDE * GROUP, SIDE * TOK), jnp.bfloat16),
             pltpu.VMEM((SIDE * GROUP, 128), jnp.float32),
-            dma((2, 3, HALF)), dma((2, 3, HALF)),
-            dma((2, SIDE, 3, HALF)), dma((2, SIDE, 3, HALF)),
-            dma((2, SIDE, 3, HALF)), dma((2, SIDE, 3, HALF)),
+            dma((RINGS, 4)), dma((RINGS, 4)),
+            dma((2, SIDE, 3, 3)), dma((2, SIDE, 3, 3)),
             dma((2, 3)), dma((2, 3)),
             dma((2, SIDE, 3)), dma((2, SIDE, 3)),
-            dma((2, SIDE, HALF)),
+            dma((2, SIDE, 3)),
         ],
         compiler_params=pltpu.CompilerParams(
             collective_id=1, has_side_effects=True, vmem_limit_bytes=VMEM_LIMIT
@@ -389,25 +470,86 @@
     )(x_rows, g_rows, hidden, gate_grad, up_grad)
 
 
+class Scatter:
+    def __init__(self, n, sems, me, dev, part, half, near_at, far_at, add):
+        self.send, self.recv = sems
+        self.n, self.me, self.dev, self.add = n, me, dev, add
+        self.part, self.half, self.near_at, self.far_at = part, half, near_at, far_at
+
+    def copy(self, src, dst, at, s):
+        return remote(src, dst, self.send.at[self.n, at], self.recv.at[self.n, at],
+                      self.dev(step(self.me, s)))
+
+    def near(self, s):
+        u = 0 if s > 0 else 1
+        return self.copy(self.part(s), self.near_at(u), u, s)
+
+    def far(self, s):
+        u = 0 if s > 0 else 1
+        return self.copy(self.half(2, u), self.far_at(u), 2 + u, s)
+
+    def first(self):
+        for s in (1, -1):
+            self.far(s).start()
+
+    def second(self, s):
+        u = 0 if s > 0 else 1
+        self.far(s).wait_recv()
+        self.add(self.half(s, u), self.far_at(u))
+        self.near(s).start()
+
+    def third(self):
+        for s in (1, -1):
+            self.near(s).wait_recv()
+
+    def drain(self):
+        for s in (1, -1):
+            self.near(s).wait_send()
+            self.far(s).wait_send()
+
+
+def add_flat(to, more):
+    width = to.shape[-1]
+
+    def tile(cols):
+        total = to[:, cols].astype(jnp.float32) + more[:, cols].astype(jnp.float32)
+        to[:, cols] = total.astype(jnp.bfloat16)
+
+    column_tiles(0, width, tile)
+
+
+def add_lines(to, more):
+    for i in range(2):
+        add_flat(to.at[i], more.at[i])
+
+
 def return_kernel(
     out_rows, grad_rows, tab_ref, mixed_ref, gtok_ref, mark_ref,
-    back0, back1, part0, part1, across0, across1, zs0, zs1, zb0, zb1, pick,
-    sa, ra, sb, rb, sc, rc, la,
+    back0, back1, pick, lpart, lnear, lfar, zpart, znear, zfar,
+    fpart0, fpart1, fnear0, fnear1, ffar0, ffar1, fsum0, fsum1, xnear0, xnear1, xfar0, xfar1,
+    gs, gr, sa, ra, la,
 ):
     ways = (Way(0), Way(1))
     rows_in = (out_rows, grad_rows)
-    back, part, across = (back0, back1), (part0, part1), (across0, across1)
-    zs, zb = (zs0, zs1), (zb0, zb1)
-    wides = (D, WIDE)
-    order = (1, 2, 3, 0)
+    back, fpart, fnear, ffar = (back0, back1), (fpart0, fpart1), (fnear0, fnear1), (ffar0, ffar1)
+    fsum, xnear, xfar = (fsum0, fsum1), (xnear0, xnear1), (xfar0, xfar1)
+    tails = (D - LATE, WIDE - LATE)
+    sems = (gs, gr)
+    both = (0, 1)
+    order = (2, 1, 3, 0)
     greet_lines()
 
-    def home(t, kk, d):
+    def piece_cols(t, piece):
+        return pl.ds(*PIECES[piece]) if piece < 2 else pl.ds(LATE, tails[t])
+
+    def home(t, kk, piece, d):
         w = ways[t]
         bs = step(w.b, kk)
         to = step(w.a, d)
-        return remote(rows_in[t].at[w.block(to, bs)], back[t].at[bs, w.a],
-                      sa.at[t, kk, d - 1], ra.at[t, kk, d - 1], w.dev(to, w.b, w.x))
+        cols = piece_cols(t, piece)
+        return remote(rows_in[t].at[w.block(to, bs), :, cols], back[t].at[bs, w.a, :, cols],
+                      sa.at[t, kk, piece, d - 1], ra.at[t, kk, piece, d - 1],
+                      w.dev(to, w.b, w.x))
 
     def stay(t, kk):
         w = ways[t]
@@ -415,105 +557,174 @@
         return pltpu.make_async_copy(rows_in[t].at[w.block(w.a, bs)], back[t].at[bs, w.a],
                                      la.at[t, kk])
 
-    def cross(t, n, kk, d):
-        w = ways[t]
-        bs = step(w.b, kk)
-        to = step(w.x, d)
-        return remote(part[t].at[n % 2, to], across[t].at[bs, w.x],
-                      sb.at[t, kk, d - 1], rb.at[t, kk, d - 1], w.dev(w.a, w.b, to))
-
-    def last(t, kk):
-        w = ways[t]
-        return remote(zs[t].at[kk - 1], zb[t].at[kk - 1], sc.at[t, kk - 1], rc.at[t, kk - 1],
-                      w.dev(w.a, step(w.b, kk), w.x))
-
     for kk in order:
-        for t in (0, 1):
-            for d in (1, 2, 3):
-                home(t, kk, d).start()
+        for t in both:
             stay(t, kk).start()
-
-    def gather_x(t, kk):
-        w = ways[t]
-        bs = step(w.b, kk)
+        for piece in range(3):
+            for t in both:
+                for d in (1, 2, 3):
+                    home(t, kk, piece, d).start()
+
+    count = iter(range(RINGS))
+
+    def along_x(t, n, kk, h):
+        w, cols = ways[t], pl.ds(*PIECES[h])
+        at = n % 2
+        return Scatter(next(count), sems, w.x, lambda i: w.dev(w.a, w.b, i),
+                       lambda o: lpart.at[t, at, step(w.x, o), :, cols],
+                       lambda o, u: lpart.at[t, at, step(w.x, o), pl.ds(u * 64, 64), cols],
+                       lambda u: lnear.at[t, kk, u, :, cols],
+                       lambda u: lfar.at[t, kk, u, :, cols], add_flat)
+
+    def along_b(t):
+        w = ways[t]
+        return Scatter(next(count), sems, w.b, lambda i: w.dev(w.a, i, w.x),
+                       lambda o: zpart.at[t, o % 4],
+                       lambda o, u: zpart.at[t, o % 4, pl.ds(u * 64, 64)],
+                       lambda u: znear.at[t, u], lambda u: zfar.at[t, u], add_flat)
+
+    def lines_b(t):
+        w = ways[t]
+        return Scatter(next(count), sems, w.b, lambda i: w.dev(w.a, i, w.x),
+                       lambda o: fpart[t].at[o % 4],
+                       lambda o, u: fpart[t].at[o % 4, pl.ds(u * 2, 2)],
+                       lambda u: fnear[t].at[u], lambda u: ffar[t].at[u], add_lines)
+
+    def late_x(t):
+        w = ways[t]
+        return Scatter(next(count), sems, w.x, lambda i: w.dev(w.a, w.b, i),
+                       lambda o: fsum[t].at[step(w.x, o)],
+                       lambda o, u: fsum[t].at[step(w.x, o), pl.ds(u * 64, 64)],
+                       lambda u: xnear[t].at[u], lambda u: xfar[t].at[u], add_flat)
+
+    x_first = [{(kk, h): along_x(t, n, kk, h) for n, kk in enumerate(order) for h in both}
+               for t in both]
+    b_then = [along_b(t) for t in both]
+    b_first = [lines_b(t) for t in both]
+    x_then = [late_x(t) for t in both]
+
+    def make_pick(t, kk):
+        tables = tab_ref[t, step(ways[t].b, kk)]
+        for a in range(SIDE):
+            hit = hits_of(tables, a)
+            weight = jnp.concatenate(lane_rows(tables, 1, a), axis=1) if t == 0 else 1.0
+            pick[a * GROUP : (a + 1) * GROUP, :] = jnp.where(hit, weight, 0.0).astype(jnp.bfloat16)
+
+    def sum_experts(t, n, kk, piece):
+        bs = step(ways[t].b, kk)
         for d in (1, 2, 3):
-            cross(t, 0, kk, d).wait_recv()
-        if kk == 0:
-            return
-
-        def total(c, _):
-            cols = pl.ds(pl.multiple_of(c * 128, 128), 128)
-            four = across[t][bs, :, :, cols].astype(jnp.float32)
-            zs[t][kk - 1, :, cols] = jnp.sum(four, axis=0).astype(jnp.bfloat16)
-            return 0
-
-        lax.fori_loop(0, wides[t] // 128, total, 0)
-        last(t, kk).start()
+            home(t, kk, piece, d).wait_recv()
+
+        def tile(cols):
+            rows = back[t][bs, :, :, cols].reshape(SIDE * GROUP, cols.size)
+            sums = contract_rows(pick[...], rows).astype(jnp.bfloat16)
+            sums = sums.reshape(SIDE, TOK, cols.size)
+            if piece < 2:
+                lpart[t, n % 2, :, :, cols] = sums
+            else:
+                fpart[t][kk, :, :, pl.ds(cols.start - LATE, cols.size)] = sums
+
+        start, width = PIECES[piece] if piece < 2 else (LATE, tails[t])
+        column_tiles(start, width, tile)
+
+    def collect_x(t, n, kk):
+        w = ways[t]
+        for h in both:
+            x_first[t][kk, h].third()
+
+        def tile(cols):
+            total = lpart[t, n % 2, w.x, :, cols].astype(jnp.float32)
+            total = total + jnp.sum(lnear[t, kk, :, :, cols].astype(jnp.float32), axis=0)
+            zpart[t, kk, :, cols] = total.astype(jnp.bfloat16)
+
+        column_tiles(0, LATE, tile)
+        if kk == 2:
+            b_then[t].first()
+        if kk in (1, 3):
+            b_then[t].second(1 if kk == 1 else -1)
 
     for n, kk in enumerate(order):
-        for t in (0, 1):
-            w = ways[t]
-            bs = step(w.b, kk)
-            tables = tab_ref[t, bs]
-            for a in range(SIDE):
-                hit = hits_of(tables, a)
-                weight = jnp.concatenate(lane_rows(tables, 1, a), axis=1) if t == 0 else 1.0
-                pick[a * GROUP : (a + 1) * GROUP, :] = jnp.where(hit, weight, 0.0).astype(
-                    jnp.bfloat16
-                )
-            for d in (1, 2, 3):
-                home(t, kk, d).wait_recv()
+        for t in both:
             stay(t, kk).wait()
+            make_pick(t, kk)
             if n >= 2:
+                for h in both:
+                    x_first[t][order[n - 2], h].drain()
+            for h in both:
+                sum_experts(t, n, kk, h)
+                x_first[t][kk, h].first()
+            sum_experts(t, n, kk, 2)
+            if kk == 2:
+                b_first[t].first()
+            if kk in (1, 3):
+                b_first[t].second(1 if kk == 1 else -1)
+        for t in both:
+            for h in both:
+                x_first[t][kk, h].second(1)
+                x_first[t][kk, h].second(-1)
+        if n >= 1:
+            for t in both:
+                collect_x(t, n - 1, order[n - 1])
+
+    for t in both:
+        b_first[t].third()
+        for i in range(SIDE):
+
+            def tile(cols, t=t, i=i):
+                total = fpart[t][0, i, :, cols].astype(jnp.float32)
+                total = total + jnp.sum(fnear[t][:, i, :, cols].astype(jnp.float32), axis=0)
+                fsum[t][i, :, cols] = total.astype(jnp.bfloat16)
+
+            column_tiles(0, tails[t], tile)
+        x_then[t].first()
+    for t in both:
+        x_then[t].second(1)
+        x_then[t].second(-1)
+    results = (mixed_ref, gtok_ref)
+    for t in both:
+        collect_x(t, 3, 0)
+        b_then[t].third()
+
+        def tile(cols, t=t):
+            total = zpart[t, 0, :, cols].astype(jnp.float32)
+            total = total + jnp.sum(znear[t, :, :, cols].astype(jnp.float32), axis=0)
+            results[t][:, cols] = total.astype(jnp.bfloat16)
+
+        column_tiles(0, LATE, tile)
+    for t in both:
+        w = ways[t]
+        x_then[t].third()
+
+        def late(cols, t=t, w=w):
+            total = fsum[t][w.x, :, cols].astype(jnp.float32)
+            return total + jnp.sum(xnear[t][:, :, cols].astype(jnp.float32), axis=0)
+
+        def tile(cols, t=t, late=late):
+            results[t][:, pl.ds(cols.start + LATE, cols.size)] = late(cols).astype(jnp.bfloat16)
+
+        column_tiles(0, D - LATE, tile)
+        if t == 1:
+            mark_ref[...] = late(pl.ds(D - LATE, 128))
+
+    for t in both:
+        for n, kk in enumerate(order):
+            for piece in range(3):
                 for d in (1, 2, 3):
-                    cross(t, n - 2, order[n - 2], d).wait_send()
-
-            def dense(c, _, t=t, bs=bs, n=n):
-                cols = pl.ds(pl.multiple_of(c * 128, 128), 128)
-                rows = back[t][bs, :, :, cols].reshape(SIDE * GROUP, 128)
-                sums = contract_rows(pick[...], rows).astype(jnp.bfloat16)
-                part[t][n % 2, :, :, cols] = sums.reshape(SIDE, TOK, 128)
-                return 0
-
-            lax.fori_loop(0, wides[t] // 128, dense, 0)
-            for d in (1, 2, 3):
-                cross(t, n, kk, d).start()
-            across[t][bs, w.x] = part[t][n % 2, w.x]
-        if n >= 1:
-            for t in (0, 1):
-                gather_x(t, order[n - 1])
-    for t in (0, 1):
-        gather_x(t, 0)
-        for kk in (1, 2, 3):
-            last(t, kk).wait_recv()
-        w = ways[t]
-
-        def finish(c, _, t=t, w=w):
-            cols = pl.ds(pl.multiple_of(c * 128, 128), 128)
-            four = jnp.sum(across[t][w.b, :, :, cols].astype(jnp.float32), axis=0)
-            rest = jnp.sum(zb[t][:, :, cols].astype(jnp.float32), axis=0)
-            (mixed_ref, gtok_ref)[t][:, cols] = (four + rest).astype(jnp.bfloat16)
-            return 0
-
-        lax.fori_loop(0, D // 128, finish, 0)
-        if t == 1:
-            marks = jnp.sum(across[1][w.b, :, :, D:].astype(jnp.float32), axis=0)
-            mark_ref[...] = marks + jnp.sum(zb[1][:, :, D:].astype(jnp.float32), axis=0)
-    for t in (0, 1):
-        for n, kk in enumerate(order):
-            for d in (1, 2, 3):
-                home(t, kk, d).wait_send()
-                if n >= 2:
-                    cross(t, n, kk, d).wait_send()
-            if kk > 0:
-                last(t, kk).wait_send()
+                    home(t, kk, piece, d).wait_send()
+            if n >= 2:
+                for h in both:
+                    x_first[t][kk, h].drain()
+        b_then[t].drain()
+        b_first[t].drain()
+        x_then[t].drain()
 
 
 def bring_back(out_rows, grad_rows, tables):
     dma = pltpu.SemaphoreType.DMA
     vmem = pl.BlockSpec(memory_space=pltpu.VMEM)
     hbm = pl.BlockSpec(memory_space=pl.ANY)
-    both = lambda lead: [pltpu.VMEM(lead + (w,), jnp.bfloat16) for w in (D, WIDE)]
+    buf = lambda *shape: pltpu.VMEM(shape, jnp.bfloat16)
+    pair = lambda *lead: [buf(*lead, D - LATE), buf(*lead, WIDE - LATE)]
     return pl.pallas_call(
         return_kernel,
         name="bring_back",
@@ -524,12 +735,15 @@
         ),
         in_specs=[hbm, hbm, vmem],
         out_specs=(vmem, vmem, vmem),
-        scratch_shapes=both((SIDE, SIDE, GROUP)) + both((2, SIDE, TOK)) + both((SIDE, SIDE, TOK))
-        + both((3, TOK)) + both((3, TOK)) + [
-            pltpu.VMEM((SIDE * GROUP, SIDE * TOK), jnp.bfloat16),
-            dma((2, SIDE, 3)), dma((2, SIDE, 3)),
-            dma((2, SIDE, 3)), dma((2, SIDE, 3)),
-            dma((2, 3)), dma((2, 3)),
+        scratch_shapes=[
+            buf(SIDE, SIDE, GROUP, D), buf(SIDE, SIDE, GROUP, WIDE),
+            buf(SIDE * GROUP, SIDE * TOK),
+            buf(2, 2, SIDE, TOK, LATE), buf(2, SIDE, 2, TOK, LATE), buf(2, SIDE, 2, TOK // 2, LATE),
+            buf(2, SIDE, TOK, LATE), buf(2, 2, TOK, LATE), buf(2, 2, TOK // 2, LATE),
+            *pair(SIDE, SIDE, TOK), *pair(2, SIDE, TOK), *pair(2, 2, TOK),
+            *pair(SIDE, TOK), *pair(2, TOK), *pair(2, TOK // 2),
+            dma((RINGS, 4)), dma((RINGS, 4)),
+            dma((2, SIDE, 3, 3)), dma((2, SIDE, 3, 3)),
             dma((2, SIDE)),
         ],
         compiler_params=pltpu.CompilerParams(

time: 524 us -> 421 us (0.80)
  Pallas kernels: 510 us -> 408 us
    pallas_call x1, Pallas kernels: 207 us -> 143 us  [dispatch(): pl.pallas_call(dispatch_kernel, name='dispatch', out_shape=(jax.ShapeDtyp...]
    pallas_call x1, Pallas kernels: 219 us -> 180 us  [bring_back(): pl.pallas_call(return_kernel, name='bring_back', out_shape=(jax.ShapeDtyp...]
where the time goes in v2:
time: 421 us; the launch traced here: 417 us
  Pallas kernels  408 us (97%)
  local copies, waits for them, and re-layouts  6.8 us (2%)
    pallas_call x1, Pallas kernels, bring_back(): pl.pallas_call(return_kernel, name='bring_back', out_shape=(jax.ShapeDtyp...  180 us
    pallas_call x1, Pallas kernels, dispatch(): pl.pallas_call(dispatch_kernel, name='dispatch', out_shape=(jax.ShapeDtyp...  143 us
    pallas_call x1, Pallas kernels, expert_rows(): pl.pallas_call(expert_kernel, name='expert_rows', grid=(ROWS // bm,), out...  47.1 us
    pallas_call x1, Pallas kernels, weight_grads(): pl.pallas_call(weight_kernel, name='weight_grads', out_shape=tuple((jax.S...  37.9 us

profile of v2, /device:TPU:2, one launch (start us, length us, event | category | flops | bytes accessed | tf_op | source)
XLA Modules:
  0.0 416.9 jit_solution(630187990029674949)
XLA Ops:
  0.6 142.8 %dispatch.1 = (bf16[16,112,2048]{2,1,0:T(8,128)(2,1)}, bf16[16,112,2048]{2,1,0:T(8,128)(2,1)}, f32[2,4,4,8,128]{4,3,2,1,0:T(8,128)}) custom-call(s32[8,128]{1,0:T(8,128)} %bitcast.15, f32[8,128]{1,0:T(8,128)} %bitcast.16, bf16[128,2048]{1,0:T(8,128)(2,1)} %tok_ref.1, bf16[128,2048]{1,0:T(8,128)(2,1)} %cot_ref.1), custom_call_target="tpu_custom_call" | custom-call | tf_op jit(solution)/shard_map/dispatch/pallas_call | solution.py:322
  143.5 47.1 %expert_rows.1 = (bf16[1792,2048]{1,0:T(8,128)(2,1)}, bf16[1792,2176]{1,0:T(8,128)(2,1)}, bf16[1792,768]{1,0:T(8,128)(2,1)}, bf16[1792,768]{1,0:T(8,128)(2,1)}, bf16[1792,768]{1,0:T(8,128)(2,1)}) custom-call(bf16[1792,2048]{1,0:T(8,128)(2,1)} %bitcast.10, bf16[1792,2048]{1,0:T(8,128)(2,1)} %bitcast.12, bf16[2048,768]{1,0:T(8,128)(2,1)} %bitcast.17, ...), custom_call_target="tpu_custom_call" | custom-call | flops 33822867456 | bytes 40000000 | tf_op jit(solution)/shard_map/expert_rows/pallas_call | solution.py:399
  190.5 0.0 copy-start.4
  190.6 0.0 copy-start.5
  190.6 179.9 %bring_back.1 = (bf16[128,2048]{1,0:T(8,128)(2,1)}, bf16[128,2048]{1,0:T(8,128)(2,1)}, f32[128,128]{1,0:T(8,128)}) custom-call(bf16[16,112,2048]{2,1,0:T(8,128)(2,1)} %bitcast.14, bf16[16,112,2176]{2,1,0:T(8,128)(2,1)} %bitcast.9, f32[2,4,4,8,128]{4,3,2,1,0:T(8,128)} %get-tuple-element.24.tab_ref), custom_call_target="tpu_custom_call" | custom-call | tf_op jit(solution)/shard_map/bring_back/pallas_call | solution.py:728
  370.5 1.0 slice_add_fusion
  371.5 0.1 copy.14
  371.6 0.0 copy-done.4
  371.6 0.0 copy-done.5
  371.7 0.6 div.3
  372.3 0.0 copy-start.3
  372.3 0.0 copy-start.2
  372.3 37.9 %weight_grads.1 = (bf16[1,2048,384]{2,1,0:T(8,128)(2,1)}, bf16[1,2048,384]{2,1,0:T(8,128)(2,1)}, bf16[1,768,1024]{2,1,0:T(8,128)(2,1)}) custom-call(bf16[1792,2048]{1,0:T(8,128)(2,1)} %bitcast.11, bf16[1792,2048]{1,0:T(8,128)(2,1)} %bitcast.13, bf16[1792,768]{1,0:T(8,128)(2,1)} %get-tuple-element.28.hid_ref, bf16[1792,768]{1,0:T(8,128)(2,1)} %get-tuple-element.29.gg_ref, ...), custom_call_target="tpu_custom_call" | custom-call | tf_op jit(solution)/shard_map/weight_grads/pallas_call | solution.py:460
  410.2 0.0 copy-start.1
  410.2 0.0 copy-done.3
  410.2 0.8 copy.20
  411.0 0.0 copy-done.2
  411.0 0.8 copy.21
  411.8 0.0 copy-start
  411.8 2.8 copy.22
  414.6 0.0 copy-done.1
  414.6 1.1 copy.23
  415.8 0.0 copy-done
  415.8 1.1 copy.24
  (1 shorter events, 0.0 us)
Async XLA Ops:
  190.5 181.1 %copy-start.4 = (s32[128,8]{0,1:T(8,128)S(1)}, s32[128,8]{0,1:T(8,128)}, u32[]{:S(2)}) copy-start(s32[128,8]{0,1:T(8,128)} %param.8) | copy-start | bytes 12292
  190.6 181.1 %copy-start.5 = (f32[128,8]{0,1:T(8,128)S(1)}, f32[128,8]{0,1:T(8,128)}, u32[]{:S(2)}) copy-start(f32[128,8]{0,1:T(8,128)} %param.9) | copy-start | bytes 12292
  372.3 37.9 %copy-start.3 = (bf16[128,2048]{1,0:T(8,128)(2,1)S(1)}, bf16[128,2048]{1,0:T(8,128)(2,1)}, u32[]{:S(2)}) copy-start(bf16[128,2048]{1,0:T(8,128)(2,1)} %get-tuple-element.40) | copy-start | bytes 1572868
  372.3 38.7 %copy-start.2 = (bf16[128,2048]{1,0:T(8,128)(2,1)S(1)}, bf16[128,2048]{1,0:T(8,128)(2,1)}, u32[]{:S(2)}) copy-start(bf16[128,2048]{1,0:T(8,128)(2,1)} %get-tuple-element.41) | copy-start | bytes 1572868
  410.2 4.4 %copy-start.1 = (bf16[1,2048,384]{2,1,0:T(8,128)(2,1)S(1)}, bf16[1,2048,384]{2,1,0:T(8,128)(2,1)}, u32[]{:S(2)}) copy-start(bf16[1,2048,384]{2,1,0:T(8,128)(2,1)} %get-tuple-element.44) | copy-start | bytes 4718596
  411.8 4.0 copy-start
